TPU v7x, 512 devices: a whole 4x8x8 slice. The times are simulated.
512 devices in a mesh: freq: 16 (over z, y_hi), strip: 32 (over x, y_lo, core).
Axes of the slice: x: 4, y: 8 (y_hi: 2, y_lo: 4; y = y_hi * 4 + y_lo), z: 8, core: 2. Of those that a mesh axis runs over, the one named last changes fastest.
Arguments:
- receiver_field: float32 [2, 16, 256, 2048], P(None, 'freq', 'strip'), may hold values from -17 to 17
- source_field: float32 [2, 16, 256, 2048], P(None, 'freq', 'strip'), may hold values from -4 to 4
- velocity_class: int32 [256, 2048], P('strip'), may hold values from 0 to 7
- filters: float32 [16, 8, 2, 9], P('freq'), may hold values from -0.8 to 0.8
- point_spread: float32 [16, 2, 15, 15], replicated, may hold values from -0.05 to 1
- spread_index: int32 [32, 16], replicated, may hold values from 0 to 15
Outputs:
- migrated: float32 [256, 2, 2048], P('strip', None, 'freq')
- reflectivity: float32 [256, 2, 2048], P('strip', None, 'freq')
- misfit: float32 [], replicated
All inputs are finite; a program needn't handle non-finite values.
Results may differ from a plain program's by a relative error of at most 0.0003.
Values sent between devices are 32-bit elements; how exact they have to be, the bound alone decides.
No kernel may reach another device: no remote copies, remote signals or barrier semaphores. Data moves between devices by JAX's collectives and lax.ppermute only.
A program may use at most 64 MiB of HBM per device.

v0:
```python
import math

import jax
import jax.numpy as jnp
from jax import lax
from jax.sharding import PartitionSpec as P

STEPS = 2
NCLASS = 8
PASSES = 2


HIGHEST = lax.Precision.HIGHEST


def extended_2(cells, sides, width):
    for axis, dim in sides:
        count = lax.axis_size(axis)
        ends = count - 1
        head = lax.slice_in_dim(cells, 0, width, axis=dim)
        tail = lax.slice_in_dim(cells, cells.shape[dim] - width, cells.shape[dim], axis=dim)
        cells = jnp.concatenate(
            [
                lax.ppermute(tail, axis, [(i, (i + 1) % count) for i in range(ends)]),
                cells,
                lax.ppermute(head, axis, [((i + 1) % count, i) for i in range(ends)]),
            ],
            axis=dim,
        )
    return cells


def class_maps(classes, filters):
    levels = jnp.arange(NCLASS, dtype=jnp.int32)
    chosen = jnp.where(classes[None] == levels[:, None, None], 1.0, 0.0)
    planes = jnp.einsum("fcpt,cxy->ptfxy", filters, chosen, precision=HIGHEST)
    taps_real = [planes[0, tap_index] for tap_index in range(9)]
    taps_imag = [planes[1, tap_index] for tap_index in range(9)]
    return (taps_real, taps_imag)


def advance(wavefield, taps_real, taps_imag, factor):
    row_count = wavefield.shape[2] - 2
    col_count = wavefield.shape[3]
    padded = jnp.pad(wavefield, ((0, 0), (0, 0), (0, 0), (1, 1)))
    real_part = jnp.zeros(taps_real[0].shape, jnp.float32)
    imag_part = jnp.zeros(taps_real[0].shape, jnp.float32)
    for tap_index in range(9):
        row_shift = tap_index // 3
        col_shift = tap_index % 3
        near_real = padded[
            0, :, row_shift : row_shift + row_count, col_shift : col_shift + col_count
        ]
        near_imag = padded[
            1, :, row_shift : row_shift + row_count, col_shift : col_shift + col_count
        ]
        coef_real = taps_real[tap_index]
        coef_imag = factor * taps_imag[tap_index]
        real_part = real_part + coef_real * near_real - coef_imag * near_imag
        imag_part = imag_part + coef_real * near_imag + coef_imag * near_real
    return jnp.stack([real_part, imag_part])


def correlate(receiver, source):
    return jnp.sum(receiver[0] * source[0] + receiver[1] * source[1], axis=0)


def lag_pick(lag_count):
    depths = jnp.arange(lag_count, dtype=jnp.int32)
    spacing = jnp.abs(depths[:, None] - depths[None, :])
    return jnp.where(spacing[None] == depths[:, None, None], 1.0, 0.0)


def convolve(extended, toeplitz, out_rows, picker):
    shifted = jnp.stack(
        [extended[shift_row : shift_row + out_rows] for shift_row in range(toeplitz.shape[0])],
        axis=2,
    )
    mixed = jnp.einsum("xdas,asly->xdly", shifted, toeplitz, precision=HIGHEST)
    return jnp.einsum("xdly,lde->xey", mixed, picker, precision=HIGHEST)


def local(receiver_field, source_field, velocity_class, filters, point_spread, spread_index):
    per_device = receiver_field.shape[1]
    row_count = receiver_field.shape[2]
    strips = lax.axis_size("strip")
    groups = lax.axis_size("freq")
    scaling = 1.0 / math.sqrt(per_device * groups)
    image_terms = []
    taps_real, taps_imag = class_maps(velocity_class, filters)
    receiver = receiver_field
    source = source_field
    for depth_step in range(STEPS):
        wide_receiver, wide_source = (
            extended_2(receiver, (("strip", 2),), 1),
            extended_2(source, (("strip", 2),), 1),
        )
        receiver = advance(wide_receiver, taps_real, taps_imag, 1.0)
        source = advance(wide_source, taps_real, taps_imag, -1.0)
        image_terms.append(correlate(receiver, source))
    partial_value = jnp.stack(image_terms, axis=1)
    whole = lax.psum(partial_value, "freq")
    share = whole.shape[2] // groups
    migrated = lax.dynamic_slice_in_dim(whole, lax.axis_index("freq") * share, share, 2)
    migrated = migrated * scaling
    col_count = migrated.shape[2]
    kernel_side = point_spread.shape[2]
    reach = kernel_side // 2
    wide_cols = col_count + 2 * reach
    picker = lag_pick(point_spread.shape[1])
    brick_row = lax.axis_index("strip")
    brick_col = lax.axis_index("freq")

    def brick_kernel(row_step, col_step):
        row_at = jnp.clip(brick_row + row_step, 0, strips - 1)
        col_at = jnp.clip(brick_col + col_step, 0, groups - 1)
        chosen = lax.dynamic_index_in_dim(
            lax.dynamic_index_in_dim(spread_index, row_at, 0, False), col_at, 0, False
        )
        return lax.dynamic_index_in_dim(point_spread, chosen, 0, False)

    columns = jnp.arange(wide_cols, dtype=jnp.int32)[:, None]
    outputs = jnp.arange(col_count, dtype=jnp.int32)[None, :]
    offsets = jnp.arange(kernel_side, dtype=jnp.int32)[:, None, None]
    band_forward = jnp.where(columns[None] - outputs[None] == offsets, 1.0, 0.0)
    band_adjoint = jnp.where(outputs[None] + 2 * reach - columns[None] == offsets, 1.0, 0.0)
    table_forward = jnp.einsum("lab,bsy->asly", brick_kernel(0, 0), band_forward, precision=HIGHEST)
    region = jnp.where(columns[:, 0] < reach, 0, jnp.where(columns[:, 0] < reach + col_count, 1, 2))
    region_pick = jnp.where(region[:, None] == jnp.arange(3, dtype=jnp.int32)[None, :], 1.0, 0.0)

    def table_adjoint(row_step):
        flipped = jnp.stack(
            [jnp.flip(brick_kernel(row_step, col_step), axis=1) for col_step in (-1, 0, 1)]
        )
        per_column = jnp.einsum("sj,jlab->slab", region_pick, flipped, precision=HIGHEST)
        return jnp.einsum("slab,bsw->aslw", per_column, band_adjoint, precision=HIGHEST)

    table_upper = table_adjoint(-1)
    table_middle = table_adjoint(0)
    table_lower = table_adjoint(1)

    def extend_rim(values):
        return extended_2(values, (("freq", 2), ("strip", 0)), reach)

    def measure(residual):
        return lax.psum(jnp.sum(residual * residual), ("freq", "strip"))

    cell_count = float(migrated.shape[1] * row_count * strips * col_count * groups)
    residual = -migrated
    reflectivity = jnp.zeros_like(migrated)
    energy = measure(residual)
    for pass_index in range(PASSES):
        weight = 1.0 / jnp.sqrt(residual * residual + energy / cell_count)
        extended = extend_rim(weight * residual)
        positions = jnp.arange(row_count + 2 * reach, dtype=jnp.int32)[:, None, None]
        middle = extended * jnp.where(
            (positions >= reach) & (positions < reach + row_count), 1.0, 0.0
        )
        summed = convolve(middle, table_middle, row_count, picker)
        upper = extended[: 3 * reach] * jnp.where(positions[: 3 * reach] < reach, 1.0, 0.0)
        lower = extended[row_count - reach :] * jnp.where(
            positions[row_count - reach :] >= row_count + reach, 1.0, 0.0
        )
        summed = summed.at[:reach].add(convolve(upper, table_upper, reach, picker))
        summed = summed.at[row_count - reach :].add(convolve(lower, table_lower, reach, picker))
        image_of = convolve(extend_rim(summed), table_forward, row_count, picker)
        grad_square, curvature = lax.psum(
            (jnp.sum(summed * summed), jnp.sum(weight * image_of * image_of)), ("freq", "strip")
        )
        step_length = grad_square / curvature
        reflectivity = reflectivity - step_length * summed
        residual = residual - step_length * image_of
        energy = measure(residual)
    return (migrated, reflectivity, energy / cell_count)


def solution(mesh):
    return jax.shard_map(
        local,
        mesh=mesh,
        in_specs=(
            P(None, "freq", "strip", None),
            P(None, "freq", "strip", None),
            P("strip", None),
            P("freq", None, None, None),
            P(),
            P(),
        ),
        out_specs=(P("strip", None, "freq"), P("strip", None, "freq"), P()),
        check_vma=False,
    )
```

profile of v0, /device:TPU:1, one launch (start us, length us, event | category | flops | bytes accessed | tf_op | source)
XLA Modules:
  0.0 950.9 jit_solution(10511014915909429593)
XLA Ops:
  8.9 4.6 collective-permute-start.2
  13.5 6.1 collective-permute-start.3
  23.1 3.0 collective-permute-start.1
  45.8 3.2 constant_dynamic-slice_fusion.2
  50.7 2.6 copy.115
  57.8 3.9 copy.109
  61.7 3.7 convolution_bitcast_fusion.2
  65.4 3.7 convolution_bitcast_fusion.3
  73.1 3.9 copy.102
  89.1 4.1 fusion.282
  93.2 2.6 collective-permute-start.6
  97.8 3.6 collective-permute-start.4
  103.8 2.7 collective-permute-done.5
  106.9 4.6 fusion.281
  112.3 5.4 convolution_bitcast_fusion.4
  117.8 193.8 %all-reduce.8.cloned.1.call-done = f32[8,2,2048]{2,1,0:T(2,128)} async-done(((f32[8,2,2048]{2,1,0:T(2,128)}), f32[8,2,2048]{2,1,0:T(2,128)}) %all-reduce.8.cloned.1.call-update) | async-done | bytes 131088 | tf_op jit(solution)/shard_map/psum | solution.py:102
  312.9 106.4 %psum.57 = f32[]{:T(128)} all-reduce(f32[]{:T(128)} %get-tuple-element.61), channel_id=1, replica_groups=mesh['freq'=16,'strip'=32] {'freq','strip'}, use_global_device_ids=true, to_apply=%region_2.3 | all-reduce | flops 1 | bytes 8 | tf_op jit(solution)/shard_map/psum | solution.py:146
  420.0 5.6 collective-permute-start.8
  427.0 7.0 collective-permute-done.9
  434.0 2.6 collective-permute-start.10
  436.7 2.8 collective-permute-start.11
  439.6 2.2 collective-permute-done.11
  442.5 4.2 fusion.14
  447.1 2.5 fusion.6
  449.5 2.5 fusion.10
  452.8 6.0 collective-permute-start.12
  462.1 5.0 collective-permute-done.13
  467.2 3.4 collective-permute-start.14
  470.5 2.1 collective-permute-start.15
  473.3 2.3 collective-permute-done.15
  476.0 2.4 fusion.2
  479.3 103.4 %all-reduce.5 = (f32[]{:T(128)}, f32[]{:T(128)}) all-reduce(f32[]{:T(128)} %multiply_reduce_fusion.2, f32[]{:T(128)} %get-tuple-element.117), channel_id=1, replica_groups=mesh['freq'=16,'strip'=32] {'freq','strip'}, use_global_device_ids=true, to_apply=%region_4.5 | all-reduce | flops 2 | bytes 16 | tf_op jit(solution)/shard_map/psum | solution.py:167
  584.6 95.3 %psum.60 = f32[]{:T(128)} all-reduce(f32[]{:T(128)} %get-tuple-element.57), channel_id=1, replica_groups=mesh['freq'=16,'strip'=32] {'freq','strip'}, use_global_device_ids=true, to_apply=%region_8.9 | all-reduce | flops 1 | bytes 8 | tf_op jit(solution)/shard_map/psum | solution.py:146
  680.6 4.8 collective-permute-start.16
  686.8 7.0 collective-permute-done.17
  693.9 2.6 collective-permute-start.18
  696.5 2.7 collective-permute-start.19
  699.2 2.3 collective-permute-done.19
  701.9 4.1 fusion.4
  706.3 2.5 fusion.8
  709.0 2.4 fusion.12
  712.4 6.5 collective-permute-start.20
  720.3 7.0 collective-permute-done.21
  727.4 3.4 collective-permute-start.22
  733.3 2.5 collective-permute-done.23
  736.2 2.4 fusion
  739.5 104.5 %all-reduce.4 = (f32[]{:T(128)}, f32[]{:T(128)}) all-reduce(f32[]{:T(128)} %multiply_reduce_fusion.1, f32[]{:T(128)} %get-tuple-element.119), channel_id=1, replica_groups=mesh['freq'=16,'strip'=32] {'freq','strip'}, use_global_device_ids=true, to_apply=%region_10.11 | all-reduce | flops 2 | bytes 16 | tf_op jit(solution)/shard_map/psum | solution.py:167
  846.6 95.3 %psum.63 = f32[]{:T(128)} all-reduce(f32[]{:T(128)} %multiply_reduce_fusion), channel_id=1, replica_groups=mesh['freq'=16,'strip'=32] {'freq','strip'}, use_global_device_ids=true, to_apply=%region_14.15 | all-reduce | flops 1 | bytes 8 | tf_op jit(solution)/shard_map/psum | solution.py:146
  (266 shorter events, 55.4 us)
Async XLA Ops:
  7.2 38.7 %copy-start.4 = (f32[16,2,15,15]{0,1,3,2:T(2,128)S(1)}, f32[16,2,15,15]{0,1,3,2:T(2,128)}, u32[]{:S(2)}) copy-start(f32[16,2,15,15]{0,1,3,2:T(2,128)} %param.18) | copy-start | bytes 86404
  7.2 304.4 %all-reduce.8.cloned.1.call-start = ((), (), s32[]{:S(2)}) async-start(), calls=%async_computation | async-start | bytes 262144 | tf_op jit(solution)/shard_map/psum | solution.py:102
  8.9 68.2 %collective-permute-start.2 = (f32[2,1,1,2048]{3,0,2,1:T(2,128)}, f32[2,1,1,2048]{3,0,2,1:T(2,128)}, u32[]{:S(2)}, u32[]{:S(2)}) collective-permute-start(f32[2,1,1,2048]{3,0,2,1:T(2,128)} %get-tuple-element.82), channel_id=1, source_target_pairs={{0,1},{1,2},{2,3},{3,4},{4,5},{5,6},{6,7},{7,8},{8,9},{9,10},{10,1... | collective-permute-start | bytes 49160 | tf_op jit(solution)/shard_map/ppermute | solution.py:24
  13.5 64.4 %collective-permute-start.3 = (f32[2,1,1,2048]{3,0,2,1:T(2,128)}, f32[2,1,1,2048]{3,0,2,1:T(2,128)}, u32[]{:S(2)}, u32[]{:S(2)}) collective-permute-start(f32[2,1,1,2048]{3,0,2,1:T(2,128)} %get-tuple-element.83), channel_id=1, source_target_pairs={{1,0},{2,1},{3,2},{4,3},{5,4},{6,5},{7,6},{8,7},{9,8},{10,9},{11,1... | collective-permute-start | bytes 49160 | tf_op jit(solution)/shard_map/ppermute | solution.py:26
  21.2 62.0 %collective-permute-start = (f32[2,1,1,2048]{3,0,2,1:T(2,128)}, f32[2,1,1,2048]{3,0,2,1:T(2,128)}, u32[]{:S(2)}, u32[]{:S(2)}) collective-permute-start(f32[2,1,1,2048]{3,0,2,1:T(2,128)} %get-tuple-element.78), channel_id=1, source_target_pairs={{0,1},{1,2},{2,3},{3,4},{4,5},{5,6},{6,7},{7,8},{8,9},{9,10},{10,1... | collective-permute-start | bytes 49160 | tf_op jit(solution)/shard_map/ppermute | solution.py:24
  23.1 61.0 %collective-permute-start.1 = (f32[2,1,1,2048]{3,0,2,1:T(2,128)}, f32[2,1,1,2048]{3,0,2,1:T(2,128)}, u32[]{:S(2)}, u32[]{:S(2)}) collective-permute-start(f32[2,1,1,2048]{3,0,2,1:T(2,128)} %get-tuple-element.79), channel_id=1, source_target_pairs={{1,0},{2,1},{3,2},{4,3},{5,4},{6,5},{7,6},{8,7},{9,8},{10,9},{11,1... | collective-permute-start | bytes 49160 | tf_op jit(solution)/shard_map/ppermute | solution.py:26
  49.1 4.3 copy-start.14
  61.7 3.7 copy-start.5
  65.4 3.8 copy-start.7
  65.4 4.1 copy-start.6
  65.4 5.8 copy-start.11
  65.4 5.8 copy-start.12
  71.2 6.6 copy-start.8
  79.6 4.3 copy-start.9
  93.2 10.1 %collective-permute-start.6 = (f32[2,1,1,2048]{3,0,2,1:T(2,128)S(1)}, f32[2,1,1,2048]{3,0,2,1:T(2,128)S(1)}, u32[]{:S(2)}, u32[]{:S(2)}) collective-permute-start(f32[2,1,1,2048]{3,0,2,1:T(2,128)S(1)} %get-tuple-element.73), channel_id=1, source_target_pairs={{0,1},{1,2},{2,3},{3,4},{4,5},{5,6},{6,7},{7,8},{8,9},{9,10},{10,1... | collective-permute-start | bytes 49160 | tf_op jit(solution)/shard_map/ppermute | solution.py:24
  95.8 7.6 collective-permute-start.7
  97.8 6.0 collective-permute-start.4
  101.4 5.1 collective-permute-start.5
  112.3 329.5 %copy-start.13 = (f32[21]{0:T(128)S(1)}, f32[21]{0:T(128)}, u32[]{:S(2)}) copy-start(f32[21]{0:T(128)} %fusion.337) | copy-start | bytes 256
  117.8 329.3 %copy-start.2 = (f32[15,142,2,128,1]{3,0,2,1,4:T(8,128)S(1)}, f32[15,142,2,128,1]{3,0,2,1,4:T(8,128)}, u32[]{:S(2)}) copy-start(f32[15,142,2,128,1]{3,0,2,1,4:T(8,128)} %convolution_bitcast_fusion.2) | copy-start | bytes 6543364
  312.9 271.1 %copy-start.10 = (f32[8,2,128]{2,1,0:T(2,128)}, f32[8,2,128]{2,1,0:T(2,128)S(1)}, u32[]{:S(2)}) copy-start(f32[8,2,128]{2,1,0:T(2,128)S(1)} %get-tuple-element.62) | copy-start | bytes 24580
  420.0 7.0 collective-permute-start.8
  425.6 8.3 collective-permute-start.9
  434.0 5.5 collective-permute-start.10
  436.7 5.0 collective-permute-start.11
  442.5 7.0 copy-start
  452.8 9.3 collective-permute-start.12
  458.7 8.3 collective-permute-start.13
  467.2 6.1 collective-permute-start.14
  470.5 5.0 collective-permute-start.15
  680.5 25.7 %copy-start.1 = (f32[15,142,2,128,1]{3,0,2,1,4:T(8,128)S(1)}, f32[15,142,2,128,1]{3,0,2,1,4:T(8,128)}, u32[]{:S(2)}) copy-start(f32[15,142,2,128,1]{3,0,2,1,4:T(8,128)} %convolution_bitcast_fusion.3) | copy-start | bytes 6543364
  680.6 6.1 collective-permute-start.16
  685.4 8.3 collective-permute-start.17
  693.9 5.3 collective-permute-start.18
  696.5 5.0 collective-permute-start.19
  706.1 2.9 copy-start.3
  712.4 7.8 collective-permute-start.20
  719.0 8.3 collective-permute-start.21
  727.4 5.9 collective-permute-start.22
  730.8 5.0 collective-permute-start.23
Sparse Core Ops, SparseCore 0:
  112.4 199.0 all-reduce.7
where the time goes:
time: 962 us; the launch traced here: 951 us
  blocking collectives  505 us (52%)
  waiting for transfers between devices  232 us (24%)
  starting transfers between devices  75.2 us (8%)
  matrix products  45.8 us (5%)
  between operations  38.4 us (4%)
  local copies, waits for them, and re-layouts  28.9 us (3%)
  other arithmetic  26 us (3%)
    psum x3, blocking collectives, measure(): return lax.psum(jnp.sum(residual * residual), ('freq', 'strip'))  297 us
    psum x2, blocking collectives, local(): lax.psum((jnp.sum(summed * summed), jnp.sum(weight * image_of * image_of)...  208 us
    psum x1, waiting for transfers between devices, local(): whole = lax.psum(partial_value, 'freq')  194 us
    ppermute x12, starting transfers between devices, extended_2(): lax.ppermute(tail, axis, [(i, (i + 1) % count) for i in range(ends)])  47.6 us
    ppermute x12, waiting for transfers between devices, extended_2(): lax.ppermute(head, axis, [((i + 1) % count, i) for i in range(ends)])  37.9 us
    ppermute x12, starting transfers between devices, extended_2(): lax.ppermute(head, axis, [((i + 1) % count, i) for i in range(ends)])  27.6 us
    dot_general x8, matrix products, convolve(): mixed = jnp.einsum('xdas,asly->xdly', shifted, toeplitz, precision=HIGHEST)  23 us
  transfers between devices with their start and end apart: 25, of which 10 were waited for; matrix products, arithmetic and copies ran while one was open for 5% of the time, Pallas kernels for 0%

commit v1 on v0

v1 whole, which is shorter than its diff:
```python
import functools
import math

import jax
import jax.numpy as jnp
from jax import lax
from jax.experimental import pallas as pl
from jax.experimental.pallas import tpu as pltpu
from jax.sharding import Mesh, PartitionSpec as P

STEPS = 2
SIDE = 15
REACH = 7
TAPS = SIDE * 16
LANES = 128
SHAPE = (8, 2, 4, 4, 2)
NAMES = ("z", "yh", "x", "yl", "c")
FREQ = ("z", "yh")
STRIP = ("x", "yl", "c")
NEAR = ("yh", "yl", "c")
FAR = ("z", "x")
GROUP = 8
CELLS = 1048576.0
ENERGY_LANE = 48

F32 = jnp.float32


def params():
    return pltpu.CompilerParams(vmem_limit_bytes=40 * 1024 * 1024)


def whole(count):
    return [pl.BlockSpec(memory_space=pltpu.VMEM)] * count


SMEM = pl.BlockSpec(memory_space=pltpu.SMEM)


def lane_iota():
    return lax.broadcasted_iota(jnp.int32, (8, LANES), 1)


def row_iota():
    return lax.broadcasted_iota(jnp.int32, (8, LANES), 0)


def pack_kernel(chunks, rec, src, cls, up, down):
    for k in range(chunks):
        at = slice(k * LANES, (k + 1) * LANES)
        for p, (field, part) in enumerate(((rec, 0), (rec, 1), (src, 0), (src, 1))):
            up[k, 2 * p : 2 * p + 2, :] = field[part, 0, 6:8, at]
            down[k, 2 * p : 2 * p + 2, :] = field[part, 0, 0:2, at]
        block, row = chunks + k // 8, k % 8
        up[block, row : row + 1, :] = cls[7:8, at].astype(F32)
        down[block, row : row + 1, :] = cls[0:1, at].astype(F32)


def pick(table, index):
    return jnp.take_along_axis(table, index, axis=1)


def image_kernel(
    chunks, place, rec, src, cls, filt, up, down, above, below, out, ext, left, right, coef, rim, img
):
    lane = lane_iota()
    row = row_iota()
    even = (row & 1) == 0
    zero = jnp.zeros((8, LANES), F32)
    first = place[0] == 0
    last = place[0] == place[2] - 1

    def tap(t):
        return jnp.broadcast_to(filt[t : t + 1, :], (8, LANES))

    for p in range(4):
        for side in (ext, left, right):
            for edge in (0, chunks + 1):
                for part in range(3):
                    side[p, edge, 8 * part : 8 * part + 8, :] = zero

    for m in range(3):
        rim[m, 0] = zero
        rim[m, chunks + 1] = zero

    def load(k, carry):
        at = pl.ds(pl.multiple_of(k * LANES, LANES), LANES)
        for p, (field, part) in enumerate(((rec, 0), (rec, 1), (src, 0), (src, 1))):
            ext[p, k + 1, 8:16, :] = field[part, 0, :, at]
            ext[p, k + 1, 0:8, :] = pltpu.roll(above[k], (6 - 2 * p) % 8, 0)
            ext[p, k + 1, 16:24, :] = pltpu.roll(below[k], (8 - 2 * p) % 8, 0)
        rim[0, k + 1] = jnp.where(even, above[k], up[k])
        rim[1, k + 1] = jnp.where(
            even, pltpu.roll(above[k], 7, 0), pltpu.roll(below[k], 1, 0)
        )
        rim[2, k + 1] = jnp.where(even, down[k], below[k])
        index = cls[:, at]
        for t in range(18):
            coef[t, k] = pick(tap(t), index)
        return carry

    lax.fori_loop(0, chunks, load, 0)

    def shift(value, before, after):
        to_right = jnp.where(lane == 0, pltpu.roll(before, 1, 1), pltpu.roll(value, 1, 1))
        to_left = jnp.where(lane == 127, pltpu.roll(after, 127, 1), pltpu.roll(value, 127, 1))
        return to_right, to_left

    def spread(k, carry):
        for p in range(4):
            for part in range(3):
                at = slice(8 * part, 8 * part + 8)
                a, b = shift(ext[p, k + 1, at, :], ext[p, k, at, :], ext[p, k + 2, at, :])
                left[p, k + 1, at, :] = a
                right[p, k + 1, at, :] = b
        return carry

    def own(k):
        parts = [None] * 4
        for t in range(9):
            plane = (left, ext, right)[t % 3]
            at = slice(7 + t // 3, 15 + t // 3)
            cr, ci = coef[t, k], coef[9 + t, k]
            rr, ri, sr, si = (plane[p, k + 1, at, :] for p in range(4))
            terms = (
                cr * rr - ci * ri,
                cr * ri + ci * rr,
                cr * sr + ci * si,
                cr * si - ci * sr,
            )
            parts = [v if q is None else q + v for q, v in zip(parts, terms)]
        return parts

    lax.fori_loop(0, chunks, spread, 0)

    def outside(k, carry):
        block = chunks + k // 8
        over = above[block, pl.ds(k % 8, 1), :]
        under = below[block, pl.ds(k % 8, 1), :]
        index = jnp.where(even, over, under).astype(jnp.int32)
        flip = jnp.where((row < 2) | (row >= 6), -1.0, 1.0)
        pair = (row & 2) == 0
        total = None
        for m in range(3):
            mid = rim[m, k + 1]
            a, b = shift(mid, rim[m, k], rim[m, k + 2])
            for n, v in enumerate((a, mid, b)):
                t = 3 * m + n
                swapped = flip * jnp.where(pair, pltpu.roll(v, 6, 0), pltpu.roll(v, 2, 0))
                term = pick(tap(t), index) * v + pick(tap(9 + t), index) * swapped
                total = term if total is None else total + term
        keep = jnp.where(even, jnp.where(first, 0.0, 1.0), jnp.where(last, 0.0, 1.0)) > 0.5
        rim[3, k + 1] = jnp.where(keep, total, 0.0)
        return carry

    lax.fori_loop(0, chunks, outside, 0)

    def step_one(k, carry):
        rr, ri, sr, si = own(k)
        img[0, k + 1] = sr * rr + si * ri
        for p, v in enumerate((rr, ri, sr, si)):
            rim[4 + p, k + 1] = v
        return carry

    lax.fori_loop(0, chunks, step_one, 0)

    def reload(k, carry):
        rows = rim[3, k + 1]
        for p in range(4):
            ext[p, k + 1, 8:16, :] = rim[4 + p, k + 1]
            ext[p, k + 1, 0:8, :] = pltpu.roll(rows, (7 - 2 * p) % 8, 0)
            ext[p, k + 1, 16:24, :] = pltpu.roll(rows, (7 - 2 * p) % 8, 0)
        return carry

    lax.fori_loop(0, chunks, reload, 0)
    lax.fori_loop(0, chunks, spread, 0)

    def step_two(k, carry):
        rr, ri, sr, si = own(k)
        img[1, k + 1] = sr * rr + si * ri
        return carry

    lax.fori_loop(0, chunks, step_two, 0)
    for d in range(STEPS):
        img[d, 0] = zero
        img[d, chunks + 1] = zero

    def give(k, carry):
        for d in range(STEPS):
            out[k, d, :, 0:LANES] = img[d, k + 1]
            out[k, d, :, LANES : 2 * LANES] = jnp.where(lane < 64, img[d, k + 2], img[d, k])
        return carry

    lax.fori_loop(0, chunks, give, 0)


def total_of(value):
    return jnp.sum(jnp.sum(value, axis=1, keepdims=True), axis=0, keepdims=True)


def sum_kernel(scaling, terms, migrated, payload):
    lane = lane_iota()
    energy = None
    halves = []
    for d in range(STEPS):
        pair = []
        for g in range(2):
            at = slice(g * LANES, (g + 1) * LANES)
            value = terms[0, d, :, at]
            for f in range(1, terms.shape[0]):
                value = value + terms[f, d, :, at]
            pair.append(value * scaling)
        migrated[:, d, :] = pair[0]
        term = pair[0] * pair[0]
        energy = term if energy is None else energy + term
        halves.append(pair)
    energy = total_of(energy)
    here = (lane >= 40) & (lane < 56)
    for d in range(STEPS):
        own = -halves[d][0]
        halo = jnp.where(here, energy, -halves[d][1])
        for n in range(payload.shape[0]):
            payload[n, d, :, 0:LANES] = own
            payload[n, d, :, LANES : 2 * LANES] = halo


def relay_kernel(place, near, energy, beside):
    total = near[0, 0, 0:1, LANES : 2 * LANES]
    for n in range(1, near.shape[0]):
        total = total + near[n, 0, 0:1, LANES : 2 * LANES]
    for n in range(energy.shape[0]):
        energy[n] = total
    start = place[3] * GROUP + jnp.where(place[4] < 4, 4, 0)
    for n in range(4):
        beside[n] = near[start + n]


def shifted(own, halo, by):
    lane = lax.broadcasted_iota(jnp.int32, own.shape, 1)
    if by == 0:
        return own, halo
    o, h = pltpu.roll(own, (-by) % LANES, 1), pltpu.roll(halo, (-by) % LANES, 1)
    near = lane < LANES - by if by > 0 else lane >= -by
    return jnp.where(near, o, h), jnp.where(near, h, o)


def table_kernel(place, index, spread, adjoint, forward):
    lane = lax.broadcasted_iota(jnp.int32, (16, LANES), 1)
    kind = lax.broadcasted_iota(jnp.int32, (16, LANES), 0)
    strips, groups = place[2], place[5]
    col = place[1]
    col_right = jnp.minimum(col + 1, groups - 1)
    col_left = jnp.maximum(col - 1, 0)
    for s in range(9):
        at = jnp.clip(place[0] + s - 4, 0, strips - 1)
        own = jnp.where(kind == index[at, col], 1.0, 0.0)
        halo = jnp.where(
            kind == jnp.where(lane < 64, index[at, col_right], index[at, col_left]), 1.0, 0.0
        )
        for sign in range(2):
            points = spread[sign]
            co = jnp.dot(points, own, precision=lax.Precision.HIGHEST, preferred_element_type=F32)
            ch = jnp.dot(points, halo, precision=lax.Precision.HIGHEST, preferred_element_type=F32)
            if 2 <= s < 7:
                forward[s - 2, 2 * sign] = co
                forward[s - 2, 2 * sign + 1] = ch
            for b in range(SIDE):
                rows = slice(16 * b, 16 * b + 16)
                so, sh = shifted(co[rows], ch[rows], REACH - b)
                adjoint[s, 2 * sign, rows, :] = so
                adjoint[s, 2 * sign + 1, rows, :] = sh


def operator_pass(count, place, resid, damping, adjoint, forward, rolled, acc, rolled_two, image):
    lane = lane_iota()
    row = row_iota()
    zero = jnp.zeros((8, LANES), F32)
    middle = count // 2

    for s in range(count):
        pairs = []
        for g in range(2):
            at = slice(g * LANES, (g + 1) * LANES)
            r0, r1 = resid[s, 0, :, at], resid[s, 1, :, at]
            u0 = r0 * (1.0 / jnp.sqrt(r0 * r0 + damping))
            u1 = r1 * (1.0 / jnp.sqrt(r1 * r1 + damping))
            pairs.append((u0 + u1, u0 - u1))
        for sign in range(2):
            for b in range(SIDE):
                o, h = shifted(pairs[0][sign], pairs[1][sign], REACH - b)
                rolled[b, 2 * sign, 8 * s : 8 * s + 8, :] = o
                rolled[b, 2 * sign + 1, 8 * s : 8 * s + 8, :] = h
    for q in range(4):
        for s in range(count + 2):
            acc[q, 8 * s : 8 * s + 8, :] = zero

    def back(s, carry):
        base = pl.multiple_of(8 * s, 8)
        for q in range(4):
            sums = [None] * SIDE
            for b in range(SIDE):
                value = rolled[b, q, pl.ds(base, 8), :]
                for a in range(SIDE):
                    r = 16 * b + a
                    term = adjoint[s, q, r : r + 1, :] * value
                    sums[a] = term if sums[a] is None else sums[a] + term
            lo, mid, hi = zero, sums[REACH], zero
            for a in range(SIDE):
                m = a - REACH
                if m == 0:
                    continue
                turned = pltpu.roll(sums[a], m % 8, 0)
                if m > 0:
                    mid = mid + jnp.where(row >= m, turned, 0.0)
                    hi = hi + jnp.where(row < m, turned, 0.0)
                else:
                    mid = mid + jnp.where(row < 8 + m, turned, 0.0)
                    lo = lo + jnp.where(row >= 8 + m, turned, 0.0)
            for n, v in enumerate((lo, mid, hi)):
                at = pl.ds(pl.multiple_of(base + 8 * n, 8), 8)
                acc[q, at, :] = acc[q, at, :] + v
        return carry

    lax.fori_loop(0, count, back, 0)

    col_ok = jnp.where(lane < 64, place[1] + 1, place[5] - place[1])
    halo_ok = col_ok < place[5]
    descent = []
    for s in range(1, count - 1):
        at = place[0] + s - middle
        row_ok = jnp.where((at >= 0) & (at < place[2]), 1.0, 0.0)
        for sign in range(2):
            o = acc[2 * sign, 8 * s + 8 : 8 * s + 16, :] * row_ok
            h = jnp.where(halo_ok, acc[2 * sign + 1, 8 * s + 8 : 8 * s + 16, :] * row_ok, 0.0)
            if s == middle:
                descent.append(o)
            for b in range(SIDE):
                so, sh = shifted(o, h, b - REACH)
                rolled_two[b, 2 * sign, 8 * s - 8 : 8 * s, :] = so
                rolled_two[b, 2 * sign + 1, 8 * s - 8 : 8 * s, :] = sh

    offset = 0 if count == 9 else 2

    def ahead(t, carry):
        base = pl.multiple_of(8 * t, 8)
        sums = [[None, None] for q in range(4)]
        for a in range(SIDE):
            for b in range(SIDE):
                r = 16 * b + a
                for q in range(4):
                    term = forward[t + offset, q, r : r + 1, :] * rolled_two[b, q, pl.ds(base + (a + 1), 8), :]
                    n = b % 2
                    sums[q][n] = term if sums[q][n] is None else sums[q][n] + term
        at = place[0] + t - (count - 4) // 2
        row_ok = jnp.where((at >= 0) & (at < place[2]), 0.5, 0.0)
        for g in range(2):
            plus = sums[g][0] + sums[g][1]
            minus = sums[2 + g][0] + sums[2 + g][1]
            q0, q1 = (plus + minus) * row_ok, (plus - minus) * row_ok
            if g == 1:
                q0, q1 = jnp.where(halo_ok, q0, 0.0), jnp.where(halo_ok, q1, 0.0)
            image[t, 0, :, g * LANES : (g + 1) * LANES] = q0
            image[t, 1, :, g * LANES : (g + 1) * LANES] = q1
        return carry

    lax.fori_loop(0, count - 4, ahead, 0)
    plus, minus = descent
    return 0.5 * (plus + minus), 0.5 * (plus - minus)


def five_sums(descent, resid, image, middle, damping, payload):
    lane = lax.broadcasted_iota(jnp.int32, (1, LANES), 1)
    sums = [jnp.zeros((8, LANES), F32)] * 5
    for d in range(STEPS):
        g, r, q = descent[d], resid[middle, d, :, 0:LANES], image[middle - 2, d, :, 0:LANES]
        w = 1.0 / jnp.sqrt(r * r + damping)
        for n, v in enumerate((g * g, w * q * q, r * q, q * q, r * r)):
            sums[n] = sums[n] + v
    value = jnp.zeros((1, LANES), F32)
    for n in range(5):
        value = jnp.where((lane >= 16 * n) & (lane < 16 * n + 16), total_of(sums[n]), value)
    for n in range(payload.shape[0]):
        payload[n] = value


def gathered(parts):
    total = parts[0]
    for n in range(1, parts.shape[0]):
        total = total + parts[n]
    return total


def at_lane(total, spot):
    lane = lax.broadcasted_iota(jnp.int32, (1, LANES), 1)
    return jnp.sum(jnp.where(lane == spot, total, 0.0), axis=1, keepdims=True)


def first_kernel(
    place, energies, near, beside, adjoint, forward, payload, resid, image, descent, energy,
    strips, rolled, acc, rolled_two,
):
    total = at_lane(gathered(energies), ENERGY_LANE)
    energy[...] = jnp.broadcast_to(total, (1, LANES))
    damping = total / CELLS
    low = jnp.where(place[4] < 4, 0, GROUP)
    base = jnp.where(place[4] < 4, 4, 0)
    for n in range(4):
        strips[low + n] = beside[n]
    for n in range(GROUP):
        strips[base + n] = near[place[3] * GROUP + n]
    start = lax.rem(place[4], 4)
    for s in range(9):
        resid[s] = strips[start + s]
    pair = operator_pass(9, place, resid, damping, adjoint, forward, rolled, acc, rolled_two, image)
    for d in range(STEPS):
        descent[d] = pair[d]
    five_sums(pair, resid, image, 4, damping, payload)


def step_and_energy(parts, energy):
    total = gathered(parts)
    square, curve, cross, image, before = (at_lane(total, 16 * n) for n in range(5))
    step = square / curve
    start = before if energy is None else energy
    after = start - 2.0 * step * cross + step * step * image
    return step, jnp.maximum(after, 0.0)


def second_kernel(
    place, parts, energy, resid_in, image_in, descent_in, adjoint, forward, payload, descent, model,
    resid, image, rolled, acc, rolled_two,
):
    step, after = step_and_energy(parts, energy[:, 0:1])
    damping = after / CELLS
    for s in range(5):
        for d in range(STEPS):
            resid[s, d] = resid_in[s + 2, d] - step * image_in[s, d]
    for d in range(STEPS):
        model[d] = -(step * descent_in[d])
    pair = operator_pass(
        5, place, resid, damping, adjoint.at[2:7], forward, rolled, acc, rolled_two, image
    )
    for d in range(STEPS):
        descent[d] = pair[d]
    five_sums(pair, resid, image, 2, damping, payload)


def last_kernel(parts, descent, model, reflectivity, misfit):
    step, after = step_and_energy(parts, None)
    for d in range(STEPS):
        reflectivity[:, d, :] = model[d] - step * descent[d]
    misfit[...] = after / CELLS


def shape(*dims):
    return jax.ShapeDtypeStruct(dims, F32)


def all_sum(parts):
    near = lax.all_to_all(parts, NEAR, 0, 0)
    total = jnp.sum(near, axis=0)
    ways = SHAPE[0] * SHAPE[2]
    return lax.all_to_all(jnp.broadcast_to(total[None], (ways, 1, LANES)), FAR, 0, 0)


def local(receiver_field, source_field, velocity_class, filters, point_spread, spread_index):
    strips = SHAPE[2] * SHAPE[3] * SHAPE[4]
    groups = SHAPE[0] * SHAPE[1]
    columns = velocity_class.shape[1]
    chunks = columns // LANES
    scaling = 1.0 / math.sqrt(groups)
    strip = lax.axis_index(STRIP)
    group = lax.axis_index(FREQ)
    half = lax.axis_index("yh")
    place = jnp.stack(
        [strip, group, jnp.int32(strips), half, lax.rem(strip, GROUP), jnp.int32(groups)]
    ).astype(jnp.int32)

    blocks = chunks + chunks // 8
    up, down = pl.pallas_call(
        functools.partial(pack_kernel, chunks),
        out_shape=(shape(blocks, 8, LANES), shape(blocks, 8, LANES)),
        in_specs=whole(3),
        out_specs=tuple(whole(2)),
        compiler_params=params(),
        name="pack",
    )(receiver_field, source_field, velocity_class)
    above = lax.ppermute(up, STRIP, [(i, i + 1) for i in range(strips - 1)])
    below = lax.ppermute(down, STRIP, [(i + 1, i) for i in range(strips - 1)])

    plus = point_spread[:, 0] + point_spread[:, 1]
    minus = point_spread[:, 0] - point_spread[:, 1]
    spread = jnp.stack([plus, minus]).transpose(0, 3, 2, 1)
    spread = jnp.pad(spread, ((0, 0), (0, 0), (0, 1), (0, 0))).reshape(2, TAPS, -1)
    adjoint, forward = pl.pallas_call(
        table_kernel,
        out_shape=(shape(9, 4, TAPS, LANES), shape(5, 4, TAPS, LANES)),
        in_specs=[SMEM, SMEM] + whole(1),
        out_specs=tuple(whole(2)),
        compiler_params=params(),
        cost_estimate=pl.CostEstimate(flops=100000000, bytes_accessed=8000000, transcendentals=0),
        name="tables",
    )(place, spread_index, spread)

    filt = filters[0].transpose(1, 2, 0).reshape(18, -1)
    filt = jnp.pad(filt, ((0, 0), (0, LANES - filt.shape[1])))
    planes = chunks + 2
    terms = pl.pallas_call(
        functools.partial(image_kernel, chunks),
        out_shape=shape(chunks, STEPS, 8, 2 * LANES),
        in_specs=[SMEM] + whole(8),
        out_specs=whole(1)[0],
        scratch_shapes=[
            pltpu.VMEM((4, planes, 24, LANES), F32),
            pltpu.VMEM((4, planes, 24, LANES), F32),
            pltpu.VMEM((4, planes, 24, LANES), F32),
            pltpu.VMEM((18, chunks, 8, LANES), F32),
            pltpu.VMEM((8, planes, 8, LANES), F32),
            pltpu.VMEM((STEPS, planes, 8, LANES), F32),
        ],
        compiler_params=params(),
        name="image",
    )(place, receiver_field, source_field, velocity_class, filt, up, down, above, below)
    terms = lax.all_to_all(terms, FREQ, 0, 0)

    nearby = SHAPE[1] * SHAPE[3] * SHAPE[4]
    far = SHAPE[0] * SHAPE[2]
    migrated, payload = pl.pallas_call(
        functools.partial(sum_kernel, scaling),
        out_shape=(shape(8, STEPS, LANES), shape(nearby, STEPS, 8, 2 * LANES)),
        in_specs=whole(1),
        out_specs=tuple(whole(2)),
        compiler_params=params(),
        name="stack",
    )(terms)
    near = lax.all_to_all(payload, NEAR, 0, 0)
    energies, beside = pl.pallas_call(
        relay_kernel,
        out_shape=(shape(far, 1, LANES), shape(4, STEPS, 8, 2 * LANES)),
        in_specs=[SMEM] + whole(1),
        out_specs=tuple(whole(2)),
        compiler_params=params(),
        name="relay",
    )(place, near)
    pairs = []
    for i in range(strips):
        to = i + GROUP if i % GROUP < 4 else i - GROUP
        if 0 <= to < strips:
            pairs.append((i, to))
    beside = lax.ppermute(beside, STRIP, pairs)
    energies = lax.all_to_all(energies, FAR, 0, 0)

    def scratch(count):
        return [
            pltpu.VMEM((SIDE, 4, 8 * count, LANES), F32),
            pltpu.VMEM((4, 8 * count + 16, LANES), F32),
            pltpu.VMEM((SIDE, 4, 8 * count - 16, LANES), F32),
        ]

    parts, resid, image, descent, energy = pl.pallas_call(
        first_kernel,
        out_shape=(
            shape(nearby, 1, LANES),
            shape(9, STEPS, 8, 2 * LANES),
            shape(5, STEPS, 8, 2 * LANES),
            shape(STEPS, 8, LANES),
            shape(1, LANES),
        ),
        in_specs=[SMEM] + whole(5),
        out_specs=tuple(whole(5)),
        scratch_shapes=[pltpu.VMEM((12, STEPS, 8, 2 * LANES), F32)] + scratch(9),
        compiler_params=params(),
        name="pass_one",
    )(place, energies, near, beside, adjoint, forward)
    parts = all_sum(parts)
    parts, descent, model = pl.pallas_call(
        second_kernel,
        out_shape=(shape(nearby, 1, LANES), shape(STEPS, 8, LANES), shape(STEPS, 8, LANES)),
        in_specs=[SMEM] + whole(7),
        out_specs=tuple(whole(3)),
        scratch_shapes=[
            pltpu.VMEM((5, STEPS, 8, 2 * LANES), F32),
            pltpu.VMEM((1, STEPS, 8, 2 * LANES), F32),
        ]
        + scratch(5),
        compiler_params=params(),
        name="pass_two",
    )(place, parts, energy, resid, image, descent, adjoint, forward)
    parts = all_sum(parts)
    reflectivity, misfit = pl.pallas_call(
        last_kernel,
        out_shape=(shape(8, STEPS, LANES), shape(1, 1)),
        in_specs=whole(3),
        out_specs=tuple(whole(2)),
        compiler_params=params(),
        name="last",
    )(parts, descent, model)
    return migrated, reflectivity, misfit.reshape(())


def solution(mesh):
    fine = Mesh(mesh.devices.reshape(SHAPE), NAMES)
    return jax.shard_map(
        local,
        mesh=fine,
        in_specs=(
            P(None, FREQ, STRIP, None),
            P(None, FREQ, STRIP, None),
            P(STRIP, None),
            P(FREQ, None, None, None),
            P(),
            P(),
        ),
        out_specs=(P(STRIP, None, FREQ), P(STRIP, None, FREQ), P()),
        check_vma=False,
    )
```

time: 962 us -> 155 us (0.16); the launches traced: 951 us -> 154 us
  blocking collectives: 505 us -> 76.2 us
  waiting for transfers between devices: 232 us -> 12.1 us
  starting transfers between devices: 75.2 us -> 25.1 us
  matrix products: 45.8 us -> 0 us
  between operations: 38.4 us -> 0.78 us
  Pallas kernels: 0 us -> 25.6 us
  other arithmetic: 26 us -> 1.62 us
  local copies, waits for them, and re-layouts: 28.9 us -> 12.9 us
    psum x5 -> x0, blocking collectives: 505 us -> none  [the longest x3 297 us: measure(): return lax.psum(jnp.sum(residual * residual), ('freq', 'strip'))]
    psum x1 -> x0, waiting for transfers between devices: 194 us -> none  [local(): whole = lax.psum(partial_value, 'freq')]
    all_to_all x0 -> x5, blocking collectives: none -> 76.2 us  [the longest x2 26.8 us: all_sum(): lax.all_to_all(jnp.broadcast_to(total[None], (ways, 1, LANES)), FAR, 0, 0)]
    ppermute x24 -> x3, starting transfers between devices: 75.2 us -> 13.2 us  [the longest x1 5.49 us: local(): below = lax.ppermute(down, STRIP, [(i + 1, i) for i in range(strips - 1)])]
    dot_general x24 -> x0, matrix products: 45.8 us -> none  [the longest x8 23 us: convolve(): mixed = jnp.einsum('xdas,asly->xdly', shifted, toeplitz, precision=HIGHEST)]
    ppermute x24 -> x3, waiting for transfers between devices: 37.9 us -> 0.01 us  [the longest x1 0.01 us: local(): above = lax.ppermute(up, STRIP, [(i, i + 1) for i in range(strips - 1)])]
    pallas_call x0 -> x8, Pallas kernels: none -> 25.6 us  [the longest x1 8.61 us: local(): pl.pallas_call(functools.partial(image_kernel, chunks), out_shape=shape(c...]
    all_to_all x0 -> x2, waiting for transfers between devices: none -> 12.1 us  [the longest x1 10.4 us: local(): near = lax.all_to_all(payload, NEAR, 0, 0)]
  transfers between devices with their start and end apart: 25 -> 5, of which waited for: 10 -> 2; matrix products, arithmetic and copies ran while one was open for 5% -> 2% of each run, Pallas kernels for 0% -> 3%
where the time goes in v1:
time: 155 us; the launch traced here: 154 us
  blocking collectives  76.2 us (49%)
  Pallas kernels  25.6 us (17%)
  starting transfers between devices  25.1 us (16%)
  local copies, waits for them, and re-layouts  12.9 us (8%)
  waiting for transfers between devices  12.1 us (8%)
  other arithmetic  1.62 us (1%)
    all_to_all x2, blocking collectives, all_sum(): lax.all_to_all(jnp.broadcast_to(total[None], (ways, 1, LANES)), FAR, 0, 0)  26.8 us
    all_to_all x1, blocking collectives, local(): terms = lax.all_to_all(terms, FREQ, 0, 0)  26.7 us
    all_to_all x2, blocking collectives, all_sum(): near = lax.all_to_all(parts, NEAR, 0, 0)  22.8 us
    unnamed x22, local copies, waits for them, and re-layouts  11.9 us
    all_to_all x1, waiting for transfers between devices, local(): near = lax.all_to_all(payload, NEAR, 0, 0)  10.4 us
    pallas_call x1, Pallas kernels, local(): pl.pallas_call(functools.partial(image_kernel, chunks), out_shape=shape(c...  8.61 us
    all_to_all x1, starting transfers between devices, local(): near = lax.all_to_all(payload, NEAR, 0, 0)  7.45 us
    pallas_call x1, Pallas kernels, local(): pl.pallas_call(first_kernel, out_shape=(shape(nearby, 1, LANES), shape(9,...  6.74 us
  transfers between devices with their start and end apart: 5, of which 2 were waited for; matrix products, arithmetic and copies ran while one was open for 2% of the time, Pallas kernels for 3%

profile of v1, /device:TPU:1, one launch (start us, length us, event | category | flops | bytes accessed | tf_op | source)
XLA Modules:
  0.0 154.3 jit_solution(16089060483218818786)
XLA Ops:
  0.6 0.0 copy-start.3
  0.6 0.9 copy-done.3
  1.5 0.0 copy-start.5
  1.5 0.9 copy-done.5
  2.4 0.0 copy-start.7
  2.4 0.8 copy-done.7
  3.3 0.0 copy-start.9
  3.3 0.1 pack.1
  3.3 4.6 %collective-permute-start = (f32[18,8,128]{2,1,0:T(8,128)S(1)}, f32[18,8,128]{2,1,0:T(8,128)S(1)}, u32[]{:S(2)}, u32[]{:S(2)}) collective-permute-start(f32[18,8,128]{2,1,0:T(8,128)S(1)} %get-tuple-element.21.up), channel_id=1, source_target_pairs={{0,1},{1,2},{2,3},{3,4},{4,5},{5,6},{6,7},{7,8},{8,9},{9,10},{10,1... | collective-permute-start | bytes 221192 | tf_op jit(solution)/shard_map/ppermute | solution.py:488
  7.9 5.5 %collective-permute-start.1 = (f32[18,8,128]{2,1,0:T(8,128)S(1)}, f32[18,8,128]{2,1,0:T(8,128)S(1)}, u32[]{:S(2)}, u32[]{:S(2)}) collective-permute-start(f32[18,8,128]{2,1,0:T(8,128)S(1)} %get-tuple-element.22.down), channel_id=1, source_target_pairs={{1,0},{2,1},{3,2},{4,3},{5,4},{6,5},{7,6},{8,7},{9,8},{10,9},{11,1... | collective-permute-start | bytes 221192 | tf_op jit(solution)/shard_map/ppermute | solution.py:489
  13.5 0.8 reshape.61
  14.2 0.1 copy.12
  14.3 0.1 stack.25.place
  14.4 0.0 collective-permute-done.above
  14.4 0.0 collective-permute-done.1.below
  14.4 0.0 copy-start.4
  14.4 0.9 copy-done.4
  15.3 0.0 copy-start.6
  15.3 0.9 copy-done.6
  16.2 0.0 copy-start.8
  16.2 0.8 copy-done.8
  17.1 8.6 %image.1 = f32[16,2,8,256]{3,2,1,0:T(8,128)S(1)} custom-call(s32[6]{0:T(128)S(1)} %stack.25.place, f32[2,1,8,2048]{3,2,1,0:T(8,128)S(1)} %copy-done.4, f32[2,1,8,2048]{3,2,1,0:T(8,128)S(1)} %copy-done.6, s32[8,2048]{1,0:T(8,128)S(1)} %copy-done.8, f32[18,128]{1,0:T(8,128)S(1)} %pad.8.filt, f32[18,8,128]{2,1,0:T(8,128)S(1)} %get-tuple-element.21.up, ...), custom_call_target="tpu_custom_call" | custom-call | tf_op jit(solution)/shard_map/image/pallas_call | solution.py:508
  25.7 26.7 %all_to_all.35.terms = f32[16,2,8,256]{3,2,1,0:T(8,128)S(1)} all-to-all(f32[16,2,8,256]{3,2,1,0:T(8,128)S(1)} %image.1), channel_id=1, replica_groups=mesh['z'=8,'yh'=2,'x'=4,'yl'=4,'c'=2] {'z','yh'}, dimensions={0} | all-to-all | bytes 524288 | tf_op jit(solution)/shard_map/all_to_all | solution.py:524
  52.4 0.8 stack.27
  53.2 7.5 %all-to-all-start.1 = ((f32[16,2,8,256]{3,2,1,0:T(8,128)}), f32[16,2,8,256]{3,2,1,0:T(8,128)S(1)}, u32[]{:S(2)}, u32[]{:S(2)}) async-start(f32[16,2,8,256]{3,2,1,0:T(8,128)} %get-tuple-element.24), calls=%async_computation.1 | async-start | bytes 524288 | tf_op jit(solution)/shard_map/all_to_all | solution.py:536
  60.6 1.3 add_bitcast_fusion
  61.9 10.4 %all-to-all-done.1.near = f32[16,2,8,256]{3,2,1,0:T(8,128)S(1)} async-done(((f32[16,2,8,256]{3,2,1,0:T(8,128)}), f32[16,2,8,256]{3,2,1,0:T(8,128)S(1)}, u32[]{:S(2)}, u32[]{:S(2)}) %all-to-all-start.1) | async-done | bytes 262176 | tf_op jit(solution)/shard_map/all_to_all | solution.py:536
  72.3 1.2 relay.1
  73.5 3.1 %collective-permute-start.2 = (f32[4,2,8,256]{3,2,1,0:T(8,128)S(1)}, f32[4,2,8,256]{3,2,1,0:T(8,128)S(1)}, u32[]{:S(2)}, u32[]{:S(2)}) collective-permute-start(f32[4,2,8,256]{3,2,1,0:T(8,128)S(1)} %get-tuple-element.26), channel_id=1, source_target_pairs={{0,8},{1,9},{2,10},{3,11},{8,16},{9,17},{10,18},{11,19},{12,4},{13... | collective-permute-start | bytes 196616 | tf_op jit(solution)/shard_map/ppermute | solution.py:550
  76.6 4.4 %all-to-all-start.2 = ((f32[32,1,128]{2,1,0:T(1,128)}), f32[32,1,128]{2,1,0:T(1,128)S(1)}, u32[]{:S(2)}, u32[]{:S(2)}) async-start(f32[32,1,128]{2,1,0:T(1,128)} %get-tuple-element.25), calls=%async_computation.2 | async-start | bytes 32768 | tf_op jit(solution)/shard_map/all_to_all | solution.py:551
  81.0 0.3 maximum_bitcast_fusion
  81.4 0.0 copy-done.9
  81.4 0.1 copy.14.index
  81.5 4.5 %tables.1 = (f32[9,4,240,128]{3,2,1,0:T(8,128)S(1)}, f32[5,4,240,128]{3,2,1,0:T(8,128)S(1)}) custom-call(s32[6]{0:T(128)S(1)} %stack.25.place, s32[32,16]{1,0:T(8,128)S(1)} %copy.14.index, f32[2,240,16]{2,1,0:T(8,128)S(1)} %bitcast.17), custom_call_target="tpu_custom_call" | custom-call | flops 100000000 | bytes 8000000 | tf_op jit(solution)/shard_map/tables/pallas_call | solution.py:495
  85.9 0.0 copy-start
  85.9 2.0 %copy-done = f32[9,4,240,128]{3,2,1,0:T(8,128)} copy-done((f32[9,4,240,128]{3,2,1,0:T(8,128)}, f32[9,4,240,128]{3,2,1,0:T(8,128)S(1)}, u32[]{:S(2)}) %copy-start) | copy-done | bytes 4423704
  88.0 1.7 %all-to-all-done.2.energies = f32[32,1,128]{2,1,0:T(1,128)S(1)} async-done(((f32[32,1,128]{2,1,0:T(1,128)}), f32[32,1,128]{2,1,0:T(1,128)S(1)}, u32[]{:S(2)}, u32[]{:S(2)}) %all-to-all-start.2) | async-done | bytes 16416 | tf_op jit(solution)/shard_map/all_to_all | solution.py:551
  89.6 0.0 collective-permute-done.2.beside
  89.6 0.0 copy-start.1
  89.6 2.3 %copy-done.1 = f32[9,4,240,128]{3,2,1,0:T(8,128)S(1)} copy-done((f32[9,4,240,128]{3,2,1,0:T(8,128)S(1)}, f32[9,4,240,128]{3,2,1,0:T(8,128)}, u32[]{:S(2)}) %copy-start.1) | copy-done | bytes 4423704
  91.9 6.7 %pass_one.1 = (f32[16,1,128]{2,1,0:T(1,128)S(1)}, f32[9,2,8,256]{3,2,1,0:T(8,128)S(1)}, f32[5,2,8,256]{3,2,1,0:T(8,128)S(1)}, f32[2,8,128]{2,1,0:T(8,128)S(1)}, f32[1,128]{1,0:T(1,128)S(1)}) custom-call(s32[6]{0:T(128)S(1)} %stack.25.place, f32[32,1,128]{2,1,0:T(1,128)S(1)} %all-to-all-done.2.energies, f32[16,2,8,256]{3,2,1,0:T(8,128)S(1)} %all-to-all-done.1.near, ...), custom_call_target="tpu_custom_call" | custom-call | tf_op jit(solution)/shard_map/pass_one/pallas_call | solution.py:560
  98.6 11.3 %all_to_all.36 = f32[16,1,128]{2,1,0:T(1,128)S(1)} all-to-all(f32[16,1,128]{2,1,0:T(1,128)S(1)} %get-tuple-element.29), channel_id=1, replica_groups=mesh['z'=8,'yh'=2,'x'=4,'yl'=4,'c'=2] {'yh','yl','c'}, dimensions={0} | all-to-all | bytes 16384 | tf_op jit(solution)/shard_map/all_to_all | solution.py:460
  109.9 15.2 %all_to_all.37.parts = f32[32,1,128]{2,1,0:T(1,128)S(1)} all-to-all(f32[32,1,128]{2,1,0:T(1,128)S(1)} %broadcast_in_dim.4), channel_id=1, replica_groups=mesh['z'=8,'yh'=2,'x'=4,'yl'=4,'c'=2] {'z','x'}, dimensions={0} | all-to-all | bytes 32768 | tf_op jit(solution)/shard_map/all_to_all | solution.py:463
  125.2 2.3 %copy-done.2 = f32[9,4,240,128]{3,2,1,0:T(8,128)S(1)} copy-done((f32[9,4,240,128]{3,2,1,0:T(8,128)S(1)}, f32[9,4,240,128]{3,2,1,0:T(8,128)}, u32[]{:S(2)}) %copy-start.2) | copy-done | bytes 4423704
  127.4 3.0 %pass_two.1 = (f32[16,1,128]{2,1,0:T(1,128)S(1)}, f32[2,8,128]{2,1,0:T(8,128)S(1)}, f32[2,8,128]{2,1,0:T(8,128)S(1)}) custom-call(s32[6]{0:T(128)S(1)} %stack.25.place, f32[32,1,128]{2,1,0:T(1,128)S(1)} %all_to_all.37.parts, f32[1,128]{1,0:T(1,128)S(1)} %get-tuple-element.30.energy, f32[9,2,8,256]{3,2,1,0:T(8,128)S(1)} %get-tuple-element.31.resid_in, ...), custom_call_target="tpu_custom_call" | custom-call | tf_op jit(solution)/shard_map/pass_two/pallas_call | solution.py:576
  130.4 11.5 %all_to_all.38 = f32[16,1,128]{2,1,0:T(1,128)S(1)} all-to-all(f32[16,1,128]{2,1,0:T(1,128)S(1)} %get-tuple-element.34), channel_id=1, replica_groups=mesh['z'=8,'yh'=2,'x'=4,'yl'=4,'c'=2] {'yh','yl','c'}, dimensions={0} | all-to-all | bytes 16384 | tf_op jit(solution)/shard_map/all_to_all | solution.py:460
  142.0 11.6 %all_to_all.39.parts = f32[32,1,128]{2,1,0:T(1,128)S(1)} all-to-all(f32[32,1,128]{2,1,0:T(1,128)S(1)} %broadcast_in_dim.5), channel_id=1, replica_groups=mesh['z'=8,'yh'=2,'x'=4,'yl'=4,'c'=2] {'z','x'}, dimensions={0} | all-to-all | bytes 32768 | tf_op jit(solution)/shard_map/all_to_all | solution.py:463
  153.5 0.7 last.1
  (8 shorter events, 0.2 us)
Async XLA Ops:
  0.6 0.9 copy-start.3
  1.5 0.9 copy-start.5
  2.4 0.8 copy-start.7
  3.3 78.1 %copy-start.9 = (s32[32,16]{0,1:T(8,128)S(1)}, s32[32,16]{0,1:T(8,128)}, u32[]{:S(2)}) copy-start(s32[32,16]{0,1:T(8,128)} %param.11) | copy-start | bytes 6148
  3.3 11.1 %collective-permute-start = (f32[18,8,128]{2,1,0:T(8,128)S(1)}, f32[18,8,128]{2,1,0:T(8,128)S(1)}, u32[]{:S(2)}, u32[]{:S(2)}) collective-permute-start(f32[18,8,128]{2,1,0:T(8,128)S(1)} %get-tuple-element.21.up), channel_id=1, source_target_pairs={{0,1},{1,2},{2,3},{3,4},{4,5},{5,6},{6,7},{7,8},{8,9},{9,10},{10,1... | collective-permute-start | bytes 221192 | tf_op jit(solution)/shard_map/ppermute | solution.py:488
  7.9 6.5 %collective-permute-start.1 = (f32[18,8,128]{2,1,0:T(8,128)S(1)}, f32[18,8,128]{2,1,0:T(8,128)S(1)}, u32[]{:S(2)}, u32[]{:S(2)}) collective-permute-start(f32[18,8,128]{2,1,0:T(8,128)S(1)} %get-tuple-element.22.down), channel_id=1, source_target_pairs={{1,0},{2,1},{3,2},{4,3},{5,4},{6,5},{7,6},{8,7},{9,8},{10,9},{11,1... | collective-permute-start | bytes 221192 | tf_op jit(solution)/shard_map/ppermute | solution.py:489
  14.4 0.9 copy-start.4
  15.3 0.9 copy-start.6
  16.2 0.8 copy-start.8
  53.2 19.2 %all-to-all-start.1 = ((f32[16,2,8,256]{3,2,1,0:T(8,128)}), f32[16,2,8,256]{3,2,1,0:T(8,128)S(1)}, u32[]{:S(2)}, u32[]{:S(2)}) async-start(f32[16,2,8,256]{3,2,1,0:T(8,128)} %get-tuple-element.24), calls=%async_computation.1 | async-start | bytes 524288 | tf_op jit(solution)/shard_map/all_to_all | solution.py:536
  73.5 16.1 %collective-permute-start.2 = (f32[4,2,8,256]{3,2,1,0:T(8,128)S(1)}, f32[4,2,8,256]{3,2,1,0:T(8,128)S(1)}, u32[]{:S(2)}, u32[]{:S(2)}) collective-permute-start(f32[4,2,8,256]{3,2,1,0:T(8,128)S(1)} %get-tuple-element.26), channel_id=1, source_target_pairs={{0,8},{1,9},{2,10},{3,11},{8,16},{9,17},{10,18},{11,19},{12,4},{13... | collective-permute-start | bytes 196616 | tf_op jit(solution)/shard_map/ppermute | solution.py:550
  76.6 13.0 %all-to-all-start.2 = ((f32[32,1,128]{2,1,0:T(1,128)}), f32[32,1,128]{2,1,0:T(1,128)S(1)}, u32[]{:S(2)}, u32[]{:S(2)}) async-start(f32[32,1,128]{2,1,0:T(1,128)} %get-tuple-element.25), calls=%async_computation.2 | async-start | bytes 32768 | tf_op jit(solution)/shard_map/all_to_all | solution.py:551
  85.9 2.0 %copy-start = (f32[9,4,240,128]{3,2,1,0:T(8,128)}, f32[9,4,240,128]{3,2,1,0:T(8,128)S(1)}, u32[]{:S(2)}) copy-start(f32[9,4,240,128]{3,2,1,0:T(8,128)S(1)} %get-tuple-element.27.adjoint) | copy-start | bytes 13271044
  89.6 2.3 %copy-start.1 = (f32[9,4,240,128]{3,2,1,0:T(8,128)S(1)}, f32[9,4,240,128]{3,2,1,0:T(8,128)}, u32[]{:S(2)}) copy-start(f32[9,4,240,128]{3,2,1,0:T(8,128)} %copy-done) | copy-start | bytes 13271044
  125.2 2.3 %copy-start.2 = (f32[9,4,240,128]{3,2,1,0:T(8,128)S(1)}, f32[9,4,240,128]{3,2,1,0:T(8,128)}, u32[]{:S(2)}) copy-start(f32[9,4,240,128]{3,2,1,0:T(8,128)} %copy-done) | copy-start | bytes 13271044

commit v2 on v1

v2 whole, which is shorter than its diff:
```python
import functools
import math

import jax
import jax.numpy as jnp
from jax import lax
from jax.experimental import pallas as pl
from jax.experimental.pallas import tpu as pltpu
from jax.sharding import Mesh, PartitionSpec as P

STEPS = 2
NCLASS = 8
SIDE = 15
REACH = 7
TAPS = SIDE * 16
LANES = 128
SHAPE = (8, 2, 4, 4, 2)
NAMES = ("z", "yh", "x", "yl", "c")
FREQ = ("z", "yh")
STRIP = ("x", "yl", "c")
NEAR = ("yh", "yl", "c")
FAR = ("z", "x")
GROUP = 8
CELLS = 1048576.0
ENERGY_LANE = 30

F32 = jnp.float32


def params(size=16):
    return pltpu.CompilerParams(vmem_limit_bytes=size * 1024 * 1024)


def whole(count):
    return [pl.BlockSpec(memory_space=pltpu.VMEM)] * count


SMEM = pl.BlockSpec(memory_space=pltpu.SMEM)
HBM = pl.BlockSpec(memory_space=pltpu.HBM)


def lane_iota():
    return lax.broadcasted_iota(jnp.int32, (8, LANES), 1)


def row_iota():
    return lax.broadcasted_iota(jnp.int32, (8, LANES), 0)


def each(count, step, by=4):
    def some(n, carry):
        for m in range(by):
            step(n * by + m)
        return carry

    lax.fori_loop(0, count // by, some, 0)


def fetch(pairs, sems):
    copies = [pltpu.make_async_copy(a, b, sems.at[n]) for n, (a, b) in enumerate(pairs)]
    for copy in copies:
        copy.start()
    for copy in copies:
        copy.wait()


def pack_kernel(
    chunks, rec_in, src_in, cls_in, up, down, field, kinds, rec, src, cls, sems
):
    fetch(((rec_in, rec), (src_in, src), (cls_in, cls)), sems)
    for k in range(chunks):
        at = slice(k * LANES, (k + 1) * LANES)
        for p, (plane, part) in enumerate(((rec, 0), (rec, 1), (src, 0), (src, 1))):
            value = plane[part, 0, :, at]
            field[p, k] = value
            up[k, 2 * p : 2 * p + 2, :] = value[6:8]
            down[k, 2 * p : 2 * p + 2, :] = value[0:2]
        block, row = chunks + k // 8, k % 8
        index = cls[:, at]
        kinds[k] = index
        up[block, row : row + 1, :] = index[7:8].astype(F32)
        down[block, row : row + 1, :] = index[0:1].astype(F32)


def pick(table, index):
    return jnp.take_along_axis(table, index, axis=1)


def tap_rows(filt, t):
    return jnp.broadcast_to(filt[t : t + 1, :], (8, LANES))


def neighbours(value, before, after):
    lane = lane_iota()
    to_right = jnp.where(lane == 0, pltpu.roll(before, 1, 1), pltpu.roll(value, 1, 1))
    to_left = jnp.where(lane == 127, pltpu.roll(after, 127, 1), pltpu.roll(value, 127, 1))
    return to_right, to_left


def inner_kernel(
    chunks, given, kinds, filters, one, two, edge, filt, field, ext, left, right, coef
):
    even = (row_iota() & 1) == 0
    zero = jnp.zeros((8, LANES), F32)
    same = lax.broadcasted_iota(jnp.int32, (9, 9), 0) == lax.broadcasted_iota(jnp.int32, (9, 9), 1)
    for part in range(2):
        filt[9 * part : 9 * part + 9, 0:NCLASS] = lax.dot_general(
            jnp.where(same, 1.0, 0.0),
            filters[0, :, part, :],
            (((1,), (1,)), ((), ())),
            precision=lax.Precision.HIGHEST,
            preferred_element_type=F32,
        )
    for p in range(4):
        for part in (0, chunks + 1):
            field[p, part] = zero

    def clear(k):
        for p in range(4):
            for side in (ext, left, right):
                side[p, k, 0:8, :] = zero
                side[p, k, 16:24, :] = zero

    each(chunks, clear)

    def load(k):
        for p in range(4):
            field[p, k + 1] = given[p, k]
        index = kinds[k]
        for t in range(18):
            coef[t, k] = pick(tap_rows(filt, t), index)
        rim = jnp.where(even, jnp.broadcast_to(index[0:1], (8, LANES)), jnp.broadcast_to(index[7:8], (8, LANES)))
        next_rim = jnp.where(even, jnp.broadcast_to(index[1:2], (8, LANES)), jnp.broadcast_to(index[6:7], (8, LANES)))
        for part in range(2):
            for n in range(3):
                t = 9 * part + n
                outward = jnp.where(even, tap_rows(filt, t), tap_rows(filt, t + 6))
                edge[3 * part + n, k] = pick(outward, rim)
                edge[6 + 3 * part + n, k] = pick(tap_rows(filt, t + 3), rim)
                edge[12 + 3 * part + n, k] = pick(outward, next_rim)

    each(chunks, load, 2)

    def spread(k):
        for p in range(4):
            value = field[p, k + 1]
            a, b = neighbours(value, field[p, k], field[p, k + 2])
            left[p, k, 8:16, :] = a
            ext[p, k, 8:16, :] = value
            right[p, k, 8:16, :] = b

    def step(out, keep, k):
        parts = [None] * 4
        for t in range(9):
            plane = (left, ext, right)[t % 3]
            at = slice(7 + t // 3, 15 + t // 3)
            cr, ci = coef[t, k], coef[9 + t, k]
            rr, ri, sr, si = (plane[p, k, at, :] for p in range(4))
            terms = (
                cr * rr - ci * ri,
                cr * ri + ci * rr,
                cr * sr + ci * si,
                cr * si - ci * sr,
            )
            parts = [v if q is None else q + v for q, v in zip(parts, terms)]
        for p in range(4):
            out[p, k] = parts[p]
            if keep:
                field[p, k + 1] = parts[p]

    each(chunks, spread)
    each(chunks, functools.partial(step, one, True), 2)
    each(chunks, spread)
    each(chunks, functools.partial(step, two, False), 2)


def edge_kernel(chunks, place, filt, one, two, edge, up, down, above, below, out, rim, img):
    lane = lane_iota()
    row = row_iota()
    even = (row & 1) == 0
    pair = (row & 2) == 0
    flip = jnp.where((row < 2) | (row >= 6), -1.0, 1.0)
    zero = jnp.zeros((8, LANES), F32)
    low = jnp.where(place[0] == 0, 0.0, 1.0)
    high = jnp.where(place[0] == place[2] - 1, 0.0, 1.0)
    keep = jnp.where(even, low, high)
    for m in range(5):
        rim[m, 0] = zero
        rim[m, chunks + 1] = zero

    def swap(v):
        return flip * jnp.where(pair, pltpu.roll(v, 6, 0), pltpu.roll(v, 2, 0))

    def near(m, k):
        mid = rim[m, k + 1]
        a, b = neighbours(mid, rim[m, k], rim[m, k + 2])
        return [(v, swap(v)) for v in (a, mid, b)]

    def load(k):
        rim[0, k + 1] = jnp.where(even, above[k], up[k])
        rim[1, k + 1] = jnp.where(even, pltpu.roll(above[k], 7, 0), pltpu.roll(below[k], 1, 0))
        rim[2, k + 1] = jnp.where(even, down[k], below[k])

    each(chunks, load)

    def first(k):
        block = chunks + k // 8
        over = above[block, pl.ds(k % 8, 1), :]
        under = below[block, pl.ds(k % 8, 1), :]
        index = jnp.where(even, over, under).astype(jnp.int32)
        total = zero
        change = zero
        for m in range(3):
            for n, (v, w) in enumerate(near(m, k)):
                t = 3 * m + n
                total = total + (pick(tap_rows(filt, t), index) * v + pick(tap_rows(filt, 9 + t), index) * w)
                if m == 1:
                    change = change + (edge[n, k] * v + edge[3 + n, k] * w)
        rim[3, k + 1] = total * keep
        rim[4, k + 1] = change

    each(chunks, first, 2)

    def second(k):
        rows, nexts = zero, zero
        for n, (v, w) in enumerate(near(3, k)):
            rows = rows + (edge[n, k] * v + edge[3 + n, k] * w)
        for n, (v, w) in enumerate(near(4, k)):
            rows = rows + (edge[6 + n, k] * v + edge[9 + n, k] * w)
            nexts = nexts + (edge[12 + n, k] * v + edge[15 + n, k] * w)
        change = rim[4, k + 1]
        turned = [[pltpu.roll(v, (first - 2 * m) % 8, 0) for m in range(4)] for v, first in ((change, 0), (rows, 0), (nexts, 1))]
        ones, twos = [], []
        for p in range(4):
            top, low_row = p, (p + 1) % 4
            ones.append(
                one[p, k]
                + jnp.where(row == 0, turned[0][top], jnp.where(row == 7, turned[0][low_row], 0.0))
            )
            outer = jnp.where(row == 0, turned[1][top], jnp.where(row == 7, turned[1][low_row], 0.0))
            inner = jnp.where(row == 1, turned[2][top], jnp.where(row == 6, turned[2][(p + 2) % 4], 0.0))
            twos.append(two[p, k] + (outer + inner))
        for d, (rr, ri, sr, si) in enumerate((ones, twos)):
            img[d, k + 1] = sr * rr + si * ri

    each(chunks, second, 2)
    for d in range(STEPS):
        img[d, 0] = zero
        img[d, chunks + 1] = zero

    outer = (lane < 32) | (lane >= 96)

    def give(k):
        sides = []
        for d in range(STEPS):
            out[k, d] = img[d, k + 1]
            sides.append(jnp.where(lane < 64, img[d, k + 2], img[d, k]))
        out[k, 2] = jnp.where(outer, sides[0], pltpu.roll(sides[1], 64, 1))

    each(chunks, give)


def total_of(value):
    return jnp.sum(jnp.sum(value, axis=1, keepdims=True), axis=0, keepdims=True)


def sum_kernel(scaling, terms, mark, migrated, payload):
    lane = lane_iota()
    values = []
    for d in range(3):
        value = terms[0, d]
        for f in range(1, terms.shape[0]):
            value = value + terms[f, d]
        values.append(value * scaling)
    for d in range(STEPS):
        migrated[:, d, :] = values[d]
    energy = total_of(values[0] * values[0] + values[1] * values[1])
    here = (lane >= 28) & (lane < 32)
    halo = jnp.where(here, energy, -values[2])
    for n in range(payload.shape[0]):
        payload[n, 0] = -values[0]
        payload[n, 1] = -values[1]
        payload[n, 2] = halo


def relay_kernel(place, near, energy, beside):
    total = near[0, 2, 0:1, :]
    for n in range(1, near.shape[0]):
        total = total + near[n, 2, 0:1, :]
    for n in range(energy.shape[0]):
        energy[n] = total
    start = place[3] * GROUP + jnp.where(place[4] < 4, 4, 0)
    for n in range(4):
        beside[n] = near[start + n]


def shifted(plus, minus, halo, by):
    if by == 0:
        return plus, minus, halo
    lane = lax.broadcasted_iota(jnp.int32, plus.shape, 1)
    turn, half = (-by) % LANES, (64 - by) % LANES
    p, m, h = (pltpu.roll(v, turn, 1) for v in (plus, minus, halo))
    m_half, h_half = pltpu.roll(minus, half, 1), pltpu.roll(halo, half, 1)
    if by > 0:
        ends, inner = lane >= LANES - by, (lane >= 64 - by) & (lane < 64)
    else:
        ends, inner = lane < -by, (lane >= 64) & (lane < 64 - by)
    return (
        jnp.where(ends, h, p),
        jnp.where(ends, h_half, m),
        jnp.where(ends, p, jnp.where(inner, m_half, h)),
    )


def halves(value):
    lane = lane_iota()
    turned = pltpu.roll(value, 64, 1)
    return jnp.where((lane < 32) | (lane >= 96), value + turned, turned - value)


def table_kernel(place, index, spread, tables_out, mark, tables, sems):
    kinds = spread.shape[1] // 2
    lane = lax.broadcasted_iota(jnp.int32, (2 * kinds, LANES), 1)
    kind = lax.broadcasted_iota(jnp.int32, (2 * kinds, LANES), 0)
    strips, groups = place[2], place[5]
    col = place[1]
    col_right = jnp.minimum(col + 1, groups - 1)
    col_left = jnp.maximum(col - 1, 0)
    points = spread[...]
    mark[...] = jnp.zeros((8, LANES), F32)
    copies = []

    def send(n):
        copy = pltpu.make_async_copy(tables.at[n], tables_out.at[n], sems.at[n])
        copy.start()
        copies.append(copy)

    for s in range(9):
        at = jnp.clip(place[0] + s - 4, 0, strips - 1)
        own = index[at, col]
        side = jnp.where((lane & 32) == 0, index[at, col_right], index[at, col_left])
        side = jnp.where((lane < 32) | (lane >= 96), side, side + kinds)
        chosen = [jnp.where(kind == v, 1.0, 0.0) for v in (own, own + kinds, side)]
        values = [
            jnp.dot(points, v, precision=lax.Precision.HIGHEST, preferred_element_type=F32)
            for v in chosen
        ]
        if 2 <= s < 7:
            for q in range(3):
                tables[7 + s, q] = values[q]
            send(7 + s)
        for b in range(SIDE):
            rows = slice(16 * b, 16 * b + 16)
            turned = shifted(*(v[rows] for v in values), REACH - b)
            for q in range(3):
                tables[s, q, rows, :] = turned[q]
        send(s)
    for copy in copies:
        copy.wait()


def table_copies(count, tables_in, tables, sems):
    skip, inner = (9 - count) // 2, 9 + (9 - count) // 2
    from_to = [(skip + n, n) for n in range(count)]
    from_to += [(inner + n, count + n) for n in range(count - 4)]
    for n, (a, b) in enumerate(from_to):
        pltpu.make_async_copy(tables_in.at[a], tables.at[b], sems.at[n]).start()

    def ready(n):
        pltpu.make_async_copy(tables_in.at[0], tables.at[n], sems.at[n]).wait()

    return ready


def operator_pass(count, place, resid, damping, tables, ready, rolled, acc, rolled_two, image):
    lane = lane_iota()
    row = row_iota()
    zero = jnp.zeros((8, LANES), F32)
    middle = count // 2

    for s in range(count):
        u0, u1, uh = (
            resid[s, n] * (1.0 / jnp.sqrt(resid[s, n] * resid[s, n] + damping)) for n in range(3)
        )
        base = (u0 + u1, u0 - u1, halves(uh))
        for b in range(SIDE):
            turned = shifted(*base, REACH - b)
            for q in range(3):
                rolled[b, q, 8 * s : 8 * s + 8, :] = turned[q]
    for q in range(3):
        for s in range(count + 2):
            acc[q, 8 * s : 8 * s + 8, :] = zero

    def back(s, carry):
        base = pl.multiple_of(8 * s, 8)
        ready(s)
        for q in range(3):
            sums = [None] * SIDE
            for b in range(SIDE):
                value = rolled[b, q, pl.ds(base, 8), :]
                for a in range(SIDE):
                    r = 16 * b + a
                    term = tables[s, q, r : r + 1, :] * value
                    sums[a] = term if sums[a] is None else sums[a] + term
            lo, mid, hi = zero, sums[REACH], zero
            for a in range(SIDE):
                m = a - REACH
                if m == 0:
                    continue
                turned = pltpu.roll(sums[a], m % 8, 0)
                if m > 0:
                    mid = mid + jnp.where(row >= m, turned, 0.0)
                    hi = hi + jnp.where(row < m, turned, 0.0)
                else:
                    mid = mid + jnp.where(row < 8 + m, turned, 0.0)
                    lo = lo + jnp.where(row >= 8 + m, turned, 0.0)
            for n, v in enumerate((lo, mid, hi)):
                at = pl.ds(pl.multiple_of(base + 8 * n, 8), 8)
                acc[q, at, :] = acc[q, at, :] + v
        return carry

    lax.fori_loop(0, count, back, 0)

    halo_ok = jnp.where((lane & 32) == 0, place[1] + 1, place[5] - place[1]) < place[5]
    descent = None
    for s in range(1, count - 1):
        at = place[0] + s - middle
        row_ok = jnp.where((at >= 0) & (at < place[2]), 1.0, 0.0)
        base = [acc[q, 8 * s + 8 : 8 * s + 16, :] * row_ok for q in range(3)]
        base[2] = jnp.where(halo_ok, base[2], 0.0)
        if s == middle:
            descent = base[:2]
        for b in range(SIDE):
            turned = shifted(*base, b - REACH)
            for q in range(3):
                rolled_two[b, q, 8 * s - 8 : 8 * s, :] = turned[q]

    def ahead(t, carry):
        base = pl.multiple_of(8 * t, 8)
        ready(count + t)
        sums = [[None, None] for q in range(3)]
        for a in range(SIDE):
            for b in range(SIDE):
                r = 16 * b + a
                for q in range(3):
                    term = tables[count + t, q, r : r + 1, :] * rolled_two[b, q, pl.ds(base + (a + 1), 8), :]
                    n = b % 2
                    sums[q][n] = term if sums[q][n] is None else sums[q][n] + term
        at = place[0] + t - (count - 4) // 2
        row_ok = jnp.where((at >= 0) & (at < place[2]), 0.5, 0.0)
        plus, minus, halo = ((v[0] + v[1]) * row_ok for v in sums)
        image[t, 0] = plus + minus
        image[t, 1] = plus - minus
        image[t, 2] = jnp.where(halo_ok, halves(halo), 0.0)
        return carry

    lax.fori_loop(0, count - 4, ahead, 0)
    plus, minus = descent
    return 0.5 * (plus + minus), 0.5 * (plus - minus)


def five_sums(descent, resid, image, middle, damping, payload):
    lane = lax.broadcasted_iota(jnp.int32, (1, LANES), 1)
    sums = [jnp.zeros((8, LANES), F32)] * 5
    for d in range(STEPS):
        g, r, q = descent[d], resid[middle, d], image[middle - 2, d]
        w = 1.0 / jnp.sqrt(r * r + damping)
        for n, v in enumerate((g * g, w * q * q, r * q, q * q, r * r)):
            sums[n] = sums[n] + v
    value = jnp.zeros((1, LANES), F32)
    for n in range(5):
        value = jnp.where((lane >= 16 * n) & (lane < 16 * n + 16), total_of(sums[n]), value)
    for n in range(payload.shape[0]):
        payload[n] = value


def gathered(parts):
    total = parts[0]
    for n in range(1, parts.shape[0]):
        total = total + parts[n]
    return total


def at_lane(total, spot):
    lane = lax.broadcasted_iota(jnp.int32, (1, LANES), 1)
    return jnp.sum(jnp.where(lane == spot, total, 0.0), axis=1, keepdims=True)


def first_kernel(
    place, energies, near, beside, tables_in, payload, state, descent, energy,
    strips, resid, image, tables, sems, rolled, acc, rolled_two,
):
    ready = table_copies(9, tables_in, tables, sems)
    total = at_lane(gathered(energies), ENERGY_LANE)
    energy[...] = jnp.broadcast_to(total, (1, LANES))
    damping = total / CELLS
    low = jnp.where(place[4] < 4, 0, GROUP)
    base = jnp.where(place[4] < 4, 4, 0)
    for n in range(4):
        strips[low + n] = beside[n]
    for n in range(GROUP):
        strips[base + n] = near[place[3] * GROUP + n]
    start = lax.rem(place[4], 4)
    for s in range(9):
        resid[s] = strips[start + s]
    pair = operator_pass(9, place, resid, damping, tables, ready, rolled, acc, rolled_two, image)
    for d in range(STEPS):
        descent[d] = pair[d]
    for s in range(5):
        state[s] = resid[s + 2]
        state[5 + s] = image[s]
    five_sums(pair, resid, image, 4, damping, payload)


def step_and_energy(parts, energy):
    total = gathered(parts)
    square, curve, cross, image, before = (at_lane(total, 16 * n) for n in range(5))
    step = square / curve
    start = before if energy is None else energy
    after = start - 2.0 * step * cross + step * step * image
    return step, jnp.maximum(after, 0.0)


def second_kernel(
    place, parts, energy, state, descent_in, tables_in, payload, descent, model,
    resid, image, tables, sems, rolled, acc, rolled_two,
):
    ready = table_copies(5, tables_in, tables, sems)
    step, after = step_and_energy(parts, energy[:, 0:1])
    damping = after / CELLS
    for s in range(5):
        for d in range(3):
            resid[s, d] = state[s, d] - step * state[5 + s, d]
    for d in range(STEPS):
        model[d] = -(step * descent_in[d])
    pair = operator_pass(5, place, resid, damping, tables, ready, rolled, acc, rolled_two, image)
    for d in range(STEPS):
        descent[d] = pair[d]
    five_sums(pair, resid, image, 2, damping, payload)


def last_kernel(parts, descent, model, reflectivity, misfit):
    step, after = step_and_energy(parts, None)
    for d in range(STEPS):
        reflectivity[:, d, :] = model[d] - step * descent[d]
    misfit[...] = after / CELLS


def shape(*dims):
    return jax.ShapeDtypeStruct(dims, F32)


def all_sum(parts):
    near = lax.all_to_all(parts, NEAR, 0, 0)
    total = jnp.sum(near, axis=0)
    ways = SHAPE[0] * SHAPE[2]
    return lax.all_to_all(jnp.broadcast_to(total[None], (ways, 1, LANES)), FAR, 0, 0)


def local(receiver_field, source_field, velocity_class, filters, point_spread, spread_index):
    strips = SHAPE[2] * SHAPE[3] * SHAPE[4]
    groups = SHAPE[0] * SHAPE[1]
    columns = velocity_class.shape[1]
    chunks = columns // LANES
    scaling = 1.0 / math.sqrt(groups)
    strip = lax.axis_index(STRIP)
    group = lax.axis_index(FREQ)
    half = lax.axis_index("yh")
    place = jnp.stack(
        [strip, group, jnp.int32(strips), half, lax.rem(strip, GROUP), jnp.int32(groups)]
    ).astype(jnp.int32)

    blocks = chunks + chunks // 8
    landing = [
        pltpu.VMEM(receiver_field.shape, F32),
        pltpu.VMEM(source_field.shape, F32),
        pltpu.VMEM(velocity_class.shape, jnp.int32),
    ]
    up, down, given, kinds = pl.pallas_call(
        functools.partial(pack_kernel, chunks),
        out_shape=(
            shape(blocks, 8, LANES),
            shape(blocks, 8, LANES),
            shape(4, chunks, 8, LANES),
            jax.ShapeDtypeStruct((chunks, 8, LANES), jnp.int32),
        ),
        in_specs=[HBM] * 3,
        out_specs=tuple(whole(4)),
        scratch_shapes=landing + [pltpu.SemaphoreType.DMA((3,))],
        compiler_params=params(16),
        name="pack",
    )(receiver_field, source_field, velocity_class)
    above = lax.ppermute(up, STRIP, [(i, i + 1) for i in range(strips - 1)])
    below = lax.ppermute(down, STRIP, [(i + 1, i) for i in range(strips - 1)])

    points = jnp.concatenate(
        [point_spread[:, 0] + point_spread[:, 1], point_spread[:, 0] - point_spread[:, 1]]
    ).transpose(2, 1, 0)
    points = jnp.pad(points, ((0, 0), (0, 1), (0, 0))).reshape(TAPS, -1)
    tables, mark = pl.pallas_call(
        table_kernel,
        out_shape=(shape(14, 3, TAPS, LANES), shape(8, LANES)),
        in_specs=[SMEM, SMEM] + whole(1),
        out_specs=(HBM, whole(1)[0]),
        scratch_shapes=[pltpu.VMEM((14, 3, TAPS, LANES), F32), pltpu.SemaphoreType.DMA((14,))],
        compiler_params=params(52),
        cost_estimate=pl.CostEstimate(flops=100000000, bytes_accessed=8000000, transcendentals=0),
        name="tables",
    )(place, spread_index, points)

    planes = chunks + 2
    one, two, edge, filt = pl.pallas_call(
        functools.partial(inner_kernel, chunks),
        out_shape=(
            shape(4, chunks, 8, LANES),
            shape(4, chunks, 8, LANES),
            shape(18, chunks, 8, LANES),
            shape(18, LANES),
        ),
        in_specs=whole(3),
        out_specs=tuple(whole(4)),
        scratch_shapes=[
            pltpu.VMEM((4, planes, 8, LANES), F32),
            pltpu.VMEM((4, chunks, 24, LANES), F32),
            pltpu.VMEM((4, chunks, 24, LANES), F32),
            pltpu.VMEM((4, chunks, 24, LANES), F32),
            pltpu.VMEM((18, chunks, 8, LANES), F32),
        ],
        compiler_params=params(),
        cost_estimate=pl.CostEstimate(flops=100000000, bytes_accessed=8000000, transcendentals=0),
        name="inner",
    )(given, kinds, filters)
    terms = pl.pallas_call(
        functools.partial(edge_kernel, chunks),
        out_shape=shape(chunks, 3, 8, LANES),
        in_specs=[SMEM] + whole(8),
        out_specs=whole(1)[0],
        scratch_shapes=[
            pltpu.VMEM((5, planes, 8, LANES), F32),
            pltpu.VMEM((STEPS, planes, 8, LANES), F32),
        ],
        compiler_params=params(),
        name="edges",
    )(place, filt, one, two, edge, up, down, above, below)
    terms = lax.all_to_all(terms, FREQ, 0, 0)

    nearby = SHAPE[1] * SHAPE[3] * SHAPE[4]
    far = SHAPE[0] * SHAPE[2]
    migrated, payload = pl.pallas_call(
        functools.partial(sum_kernel, scaling),
        out_shape=(shape(8, STEPS, LANES), shape(nearby, 3, 8, LANES)),
        in_specs=whole(2),
        out_specs=tuple(whole(2)),
        compiler_params=params(),
        name="stack",
    )(terms, mark)
    near = lax.all_to_all(payload, NEAR, 0, 0)
    energies, beside = pl.pallas_call(
        relay_kernel,
        out_shape=(shape(far, 1, LANES), shape(4, 3, 8, LANES)),
        in_specs=[SMEM] + whole(1),
        out_specs=tuple(whole(2)),
        compiler_params=params(),
        name="relay",
    )(place, near)
    pairs = []
    for i in range(strips):
        to = i + GROUP if i % GROUP < 4 else i - GROUP
        if 0 <= to < strips:
            pairs.append((i, to))
    beside = lax.ppermute(beside, STRIP, pairs)
    energies = lax.all_to_all(energies, FAR, 0, 0)

    def scratch(count):
        return [
            pltpu.VMEM((count, 3, 8, LANES), F32),
            pltpu.VMEM((count - 4, 3, 8, LANES), F32),
            pltpu.VMEM((2 * count - 4, 3, TAPS, LANES), F32),
            pltpu.SemaphoreType.DMA((2 * count - 4,)),
            pltpu.VMEM((SIDE, 3, 8 * count, LANES), F32),
            pltpu.VMEM((3, 8 * count + 16, LANES), F32),
            pltpu.VMEM((SIDE, 3, 8 * count - 16, LANES), F32),
        ]

    parts, state, descent, energy = pl.pallas_call(
        first_kernel,
        out_shape=(
            shape(nearby, 1, LANES),
            shape(10, 3, 8, LANES),
            shape(STEPS, 8, LANES),
            shape(1, LANES),
        ),
        in_specs=[SMEM] + whole(3) + [HBM],
        out_specs=tuple(whole(4)),
        scratch_shapes=[pltpu.VMEM((12, 3, 8, LANES), F32)] + scratch(9),
        compiler_params=params(52),
        name="pass_one",
    )(place, energies, near, beside, tables)
    parts = all_sum(parts)
    parts, descent, model = pl.pallas_call(
        second_kernel,
        out_shape=(shape(nearby, 1, LANES), shape(STEPS, 8, LANES), shape(STEPS, 8, LANES)),
        in_specs=[SMEM] + whole(4) + [HBM],
        out_specs=tuple(whole(3)),
        scratch_shapes=scratch(5),
        compiler_params=params(52),
        name="pass_two",
    )(place, parts, energy, state, descent, tables)
    parts = all_sum(parts)
    reflectivity, misfit = pl.pallas_call(
        last_kernel,
        out_shape=(shape(8, STEPS, LANES), shape(1, 1)),
        in_specs=whole(3),
        out_specs=tuple(whole(2)),
        compiler_params=params(),
        name="last",
    )(parts, descent, model)
    return migrated, reflectivity, misfit.reshape(())


def solution(mesh):
    fine = Mesh(mesh.devices.reshape(SHAPE), NAMES)
    return jax.shard_map(
        local,
        mesh=fine,
        in_specs=(
            P(None, FREQ, STRIP, None),
            P(None, FREQ, STRIP, None),
            P(STRIP, None),
            P(FREQ, None, None, None),
            P(),
            P(),
        ),
        out_specs=(P(STRIP, None, FREQ), P(STRIP, None, FREQ), P()),
        check_vma=False,
    )
```

time: 155 us -> 142 us (0.916)
  local copies, waits for them, and re-layouts: 12.9 us -> 6 us
  waiting for transfers between devices: 12.1 us -> 5.7 us
  blocking collectives: 76.2 us -> 78.3 us
    unnamed x22 -> x12, local copies, waits for them, and re-layouts: 11.9 us -> 4.61 us
    all_to_all x2 -> x1, waiting for transfers between devices: 12.1 us -> 5.69 us  [local(): terms = lax.all_to_all(terms, FREQ, 0, 0)]
    all_to_all x1 -> x2, blocking collectives: 26.7 us -> 32.5 us  [the longest x1 16.8 us: local(): near = lax.all_to_all(payload, NEAR, 0, 0)]
    all_to_all x2, blocking collectives: 26.8 us -> 23.1 us  [all_sum(): lax.all_to_all(jnp.broadcast_to(total[None], (ways, 1, LANES)), FAR, 0, 0)]
    pallas_call x4 -> x5, Pallas kernels: 21 us -> 19.9 us  [the longest x1 7.62 us: local(): pl.pallas_call(first_kernel, out_shape=(shape(nearby, 1, LANES), shape(10...]
    all_to_all x2 -> x1, starting transfers between devices: 11.9 us -> 10.9 us  [local(): terms = lax.all_to_all(terms, FREQ, 0, 0)]
  transfers between devices with their start and end apart: 5 -> 4, of which waited for: 2 -> 1; matrix products, arithmetic and copies ran while one was open for 2% -> 2% of each run, Pallas kernels for 3% -> 6%
where the time goes in v2:
time: 142 us; the launch traced here: 141 us
  blocking collectives  78.3 us (55%)
  Pallas kernels  25.6 us (18%)
  starting transfers between devices  24.9 us (18%)
  local copies, waits for them, and re-layouts  6 us (4%)
  waiting for transfers between devices  5.7 us (4%)
    all_to_all x2, blocking collectives, all_sum(): lax.all_to_all(jnp.broadcast_to(total[None], (ways, 1, LANES)), FAR, 0, 0)  23.1 us
    all_to_all x2, blocking collectives, all_sum(): near = lax.all_to_all(parts, NEAR, 0, 0)  22.6 us
    all_to_all x1, blocking collectives, local(): near = lax.all_to_all(payload, NEAR, 0, 0)  16.8 us
    all_to_all x1, blocking collectives, local(): energies = lax.all_to_all(energies, FAR, 0, 0)  15.7 us
    all_to_all x1, starting transfers between devices, local(): terms = lax.all_to_all(terms, FREQ, 0, 0)  10.9 us
    pallas_call x1, Pallas kernels, local(): pl.pallas_call(first_kernel, out_shape=(shape(nearby, 1, LANES), shape(10...  7.62 us
    all_to_all x1, waiting for transfers between devices, local(): terms = lax.all_to_all(terms, FREQ, 0, 0)  5.69 us
    ppermute x1, starting transfers between devices, local(): below = lax.ppermute(down, STRIP, [(i + 1, i) for i in range(strips - 1)])  5.49 us
  transfers between devices with their start and end apart: 4, of which 1 were waited for; matrix products, arithmetic and copies ran while one was open for 2% of the time, Pallas kernels for 6%

profile of v2, /device:TPU:1, one launch (start us, length us, event | category | flops | bytes accessed | tf_op | source)
XLA Modules:
  0.0 141.3 jit_solution(14900684451947902220)
XLA Ops:
  0.6 0.0 copy-start
  0.6 0.9 copy-done
  1.5 0.0 copy-start.1
  1.5 0.9 copy-done.1
  2.4 0.0 copy-start.2
  2.4 0.8 copy-done.2
  3.3 0.5 pack.1
  3.8 4.6 %collective-permute-start = (f32[18,8,128]{2,1,0:T(8,128)S(1)}, f32[18,8,128]{2,1,0:T(8,128)S(1)}, u32[]{:S(2)}, u32[]{:S(2)}) collective-permute-start(f32[18,8,128]{2,1,0:T(8,128)S(1)} %get-tuple-element.32.up), channel_id=1, source_target_pairs={{0,1},{1,2},{2,3},{3,4},{4,5},{5,6},{6,7},{7,8},{8,9},{9,10},{10,1... | collective-permute-start | bytes 221192 | tf_op jit(solution)/shard_map/ppermute | solution.py:593
  8.4 5.5 %collective-permute-start.1 = (f32[18,8,128]{2,1,0:T(8,128)S(1)}, f32[18,8,128]{2,1,0:T(8,128)S(1)}, u32[]{:S(2)}, u32[]{:S(2)}) collective-permute-start(f32[18,8,128]{2,1,0:T(8,128)S(1)} %get-tuple-element.33.down), channel_id=1, source_target_pairs={{1,0},{2,1},{3,2},{4,3},{5,4},{6,5},{7,6},{8,7},{9,8},{10,9},{11,1... | collective-permute-start | bytes 221192 | tf_op jit(solution)/shard_map/ppermute | solution.py:594
  13.9 0.1 stack.20.place
  14.0 0.0 copy-start.3
  14.0 0.7 copy-done.3
  14.7 3.6 %inner.1 = (f32[4,16,8,128]{3,2,1,0:T(8,128)S(1)}, f32[4,16,8,128]{3,2,1,0:T(8,128)S(1)}, f32[18,16,8,128]{3,2,1,0:T(8,128)S(1)}, f32[18,128]{1,0:T(8,128)S(1)}) custom-call(f32[4,16,8,128]{3,2,1,0:T(8,128)S(1)} %get-tuple-element.26.given, s32[16,8,128]{2,1,0:T(8,128)S(1)} %get-tuple-element.27.kinds, f32[1,8,2,9]{3,2,1,0:T(2,128)S(1)} %copy-done.3), custom_call_target="tpu_custom_call" | custom-call | flops 100000000 | bytes 8000000 | tf_op jit(solution)/shard_map/inner/pallas_call | solution.py:612
  18.3 0.0 collective-permute-done.above
  18.3 0.0 collective-permute-done.1.below
  18.3 3.5 %edges.1 = f32[16,3,8,128]{3,2,1,0:T(8,128)} custom-call(s32[6]{0:T(128)S(1)} %stack.20.place, f32[18,128]{1,0:T(8,128)S(1)} %get-tuple-element.28.filt, f32[4,16,8,128]{3,2,1,0:T(8,128)S(1)} %get-tuple-element.29.one, f32[4,16,8,128]{3,2,1,0:T(8,128)S(1)} %get-tuple-element.30.two, f32[18,16,8,128]{3,2,1,0:T(8,128)S(1)} %get-tuple-element.31.edge, ...), custom_call_target="tpu_custom_call" | custom-call | tf_op jit(solution)/shard_map/edges/pallas_call | solution.py:633
  21.9 10.9 %all-to-all-start = ((f32[16,3,8,128]{3,2,1,0:T(8,128)}), f32[16,3,8,128]{3,2,1,0:T(8,128)S(1)}, u32[]{:S(2)}, u32[]{:S(2)}) async-start(f32[16,3,8,128]{3,2,1,0:T(8,128)} %edges.1), calls=%async_computation | async-start | bytes 393216 | tf_op jit(solution)/shard_map/all_to_all | solution.py:645
  32.8 1.3 fusion
  34.1 0.8 copy.17.index
  34.8 0.2 copy.19
  35.0 0.2 copy.18
  35.2 0.2 copy.20
  35.4 4.6 %tables.1 = (f32[14,3,240,128]{3,2,1,0:T(8,128)}, f32[8,128]{1,0:T(8,128)S(1)}) custom-call(s32[6]{0:T(128)S(1)} %stack.20.place, s32[32,16]{1,0:T(8,128)S(1)} %copy.17.index, f32[240,32]{1,0:T(8,128)S(1)} %bitcast.12), custom_call_target="tpu_custom_call" | custom-call | flops 100000000 | bytes 8000000 | tf_op jit(solution)/shard_map/tables/pallas_call | solution.py:600
  40.0 5.7 %all-to-all-done.terms = f32[16,3,8,128]{3,2,1,0:T(8,128)S(1)} async-done(((f32[16,3,8,128]{3,2,1,0:T(8,128)}), f32[16,3,8,128]{3,2,1,0:T(8,128)S(1)}, u32[]{:S(2)}, u32[]{:S(2)}) %all-to-all-start) | async-done | bytes 196640 | tf_op jit(solution)/shard_map/all_to_all | solution.py:645
  45.7 0.6 stack.21
  46.3 16.8 %all_to_all.35.near = f32[16,3,8,128]{3,2,1,0:T(8,128)S(1)} all-to-all(f32[16,3,8,128]{3,2,1,0:T(8,128)S(1)} %get-tuple-element.36), channel_id=1, replica_groups=mesh['z'=8,'yh'=2,'x'=4,'yl'=4,'c'=2] {'yh','yl','c'}, dimensions={0} | all-to-all | bytes 393216 | tf_op jit(solution)/shard_map/all_to_all | solution.py:657
  63.2 0.6 relay.1
  63.7 3.9 %collective-permute-start.2 = (f32[4,3,8,128]{3,2,1,0:T(8,128)S(1)}, f32[4,3,8,128]{3,2,1,0:T(8,128)S(1)}, u32[]{:S(2)}, u32[]{:S(2)}) collective-permute-start(f32[4,3,8,128]{3,2,1,0:T(8,128)S(1)} %get-tuple-element.38), channel_id=1, source_target_pairs={{0,8},{1,9},{2,10},{3,11},{8,16},{9,17},{10,18},{11,19},{12,4},{13... | collective-permute-start | bytes 147464 | tf_op jit(solution)/shard_map/ppermute | solution.py:671
  67.6 15.7 %all_to_all.36.energies = f32[32,1,128]{2,1,0:T(1,128)S(1)} all-to-all(f32[32,1,128]{2,1,0:T(1,128)S(1)} %get-tuple-element.37), channel_id=1, replica_groups=mesh['z'=8,'yh'=2,'x'=4,'yl'=4,'c'=2] {'z','x'}, dimensions={0} | all-to-all | bytes 32768 | tf_op jit(solution)/shard_map/all_to_all | solution.py:672
  83.3 0.0 collective-permute-done.2.beside
  83.3 7.6 %pass_one.1 = (f32[16,1,128]{2,1,0:T(1,128)S(1)}, f32[10,3,8,128]{3,2,1,0:T(8,128)S(1)}, f32[2,8,128]{2,1,0:T(8,128)S(1)}, f32[1,128]{1,0:T(1,128)S(1)}) custom-call(s32[6]{0:T(128)S(1)} %stack.20.place, f32[32,1,128]{2,1,0:T(1,128)S(1)} %all_to_all.36.energies, f32[16,3,8,128]{3,2,1,0:T(8,128)S(1)} %all_to_all.35.near, ...), custom_call_target="tpu_custom_call" | custom-call | tf_op jit(solution)/shard_map/pass_one/pallas_call | solution.py:685
  90.9 11.4 %all_to_all.37 = f32[16,1,128]{2,1,0:T(1,128)S(1)} all-to-all(f32[16,1,128]{2,1,0:T(1,128)S(1)} %get-tuple-element.40), channel_id=1, replica_groups=mesh['z'=8,'yh'=2,'x'=4,'yl'=4,'c'=2] {'yh','yl','c'}, dimensions={0} | all-to-all | bytes 16384 | tf_op jit(solution)/shard_map/all_to_all | solution.py:554
  102.4 11.6 %all_to_all.38.parts = f32[32,1,128]{2,1,0:T(1,128)S(1)} all-to-all(f32[32,1,128]{2,1,0:T(1,128)S(1)} %broadcast_in_dim.4), channel_id=1, replica_groups=mesh['z'=8,'yh'=2,'x'=4,'yl'=4,'c'=2] {'z','x'}, dimensions={0} | all-to-all | bytes 32768 | tf_op jit(solution)/shard_map/all_to_all | solution.py:557
  113.9 3.8 %pass_two.1 = (f32[16,1,128]{2,1,0:T(1,128)S(1)}, f32[2,8,128]{2,1,0:T(8,128)S(1)}, f32[2,8,128]{2,1,0:T(8,128)S(1)}) custom-call(s32[6]{0:T(128)S(1)} %stack.20.place, f32[32,1,128]{2,1,0:T(1,128)S(1)} %all_to_all.38.parts, f32[1,128]{1,0:T(1,128)S(1)} %get-tuple-element.41.energy, f32[10,3,8,128]{3,2,1,0:T(8,128)S(1)} %get-tuple-element.42.state, ...), custom_call_target="tpu_custom_call" | custom-call | tf_op jit(solution)/shard_map/pass_two/pallas_call | solution.py:700
  117.7 11.2 %all_to_all.39 = f32[16,1,128]{2,1,0:T(1,128)S(1)} all-to-all(f32[16,1,128]{2,1,0:T(1,128)S(1)} %get-tuple-element.44), channel_id=1, replica_groups=mesh['z'=8,'yh'=2,'x'=4,'yl'=4,'c'=2] {'yh','yl','c'}, dimensions={0} | all-to-all | bytes 16384 | tf_op jit(solution)/shard_map/all_to_all | solution.py:554
  129.0 11.6 %all_to_all.40.parts = f32[32,1,128]{2,1,0:T(1,128)S(1)} all-to-all(f32[32,1,128]{2,1,0:T(1,128)S(1)} %broadcast_in_dim.5), channel_id=1, replica_groups=mesh['z'=8,'yh'=2,'x'=4,'yl'=4,'c'=2] {'z','x'}, dimensions={0} | all-to-all | bytes 32768 | tf_op jit(solution)/shard_map/all_to_all | solution.py:557
  140.6 0.7 last.1
  (7 shorter events, 0.2 us)
Async XLA Ops:
  0.6 0.9 copy-start
  1.5 0.9 copy-start.1
  2.4 0.8 copy-start.2
  3.8 14.5 %collective-permute-start = (f32[18,8,128]{2,1,0:T(8,128)S(1)}, f32[18,8,128]{2,1,0:T(8,128)S(1)}, u32[]{:S(2)}, u32[]{:S(2)}) collective-permute-start(f32[18,8,128]{2,1,0:T(8,128)S(1)} %get-tuple-element.32.up), channel_id=1, source_target_pairs={{0,1},{1,2},{2,3},{3,4},{4,5},{5,6},{6,7},{7,8},{8,9},{9,10},{10,1... | collective-permute-start | bytes 221192 | tf_op jit(solution)/shard_map/ppermute | solution.py:593
  8.4 9.9 %collective-permute-start.1 = (f32[18,8,128]{2,1,0:T(8,128)S(1)}, f32[18,8,128]{2,1,0:T(8,128)S(1)}, u32[]{:S(2)}, u32[]{:S(2)}) collective-permute-start(f32[18,8,128]{2,1,0:T(8,128)S(1)} %get-tuple-element.33.down), channel_id=1, source_target_pairs={{1,0},{2,1},{3,2},{4,3},{5,4},{6,5},{7,6},{8,7},{9,8},{10,9},{11,1... | collective-permute-start | bytes 221192 | tf_op jit(solution)/shard_map/ppermute | solution.py:594
  14.0 0.7 copy-start.3
  21.9 23.8 %all-to-all-start = ((f32[16,3,8,128]{3,2,1,0:T(8,128)}), f32[16,3,8,128]{3,2,1,0:T(8,128)S(1)}, u32[]{:S(2)}, u32[]{:S(2)}) async-start(f32[16,3,8,128]{3,2,1,0:T(8,128)} %edges.1), calls=%async_computation | async-start | bytes 393216 | tf_op jit(solution)/shard_map/all_to_all | solution.py:645
  63.7 19.6 %collective-permute-start.2 = (f32[4,3,8,128]{3,2,1,0:T(8,128)S(1)}, f32[4,3,8,128]{3,2,1,0:T(8,128)S(1)}, u32[]{:S(2)}, u32[]{:S(2)}) collective-permute-start(f32[4,3,8,128]{3,2,1,0:T(8,128)S(1)} %get-tuple-element.38), channel_id=1, source_target_pairs={{0,8},{1,9},{2,10},{3,11},{8,16},{9,17},{10,18},{11,19},{12,4},{13... | collective-permute-start | bytes 147464 | tf_op jit(solution)/shard_map/ppermute | solution.py:671

commit v3 on v2

--- a/solution.py
+++ b/solution.py
@@ -47,13 +47,9 @@
     return lax.broadcasted_iota(jnp.int32, (8, LANES), 0)
 
 
-def each(count, step, by=4):
-    def some(n, carry):
-        for m in range(by):
-            step(n * by + m)
-        return carry
-
-    lax.fori_loop(0, count // by, some, 0)
+def each(count, step):
+    for k in range(count):
+        step(k)
 
 
 def fetch(pairs, sems):
@@ -65,21 +61,23 @@
 
 
 def pack_kernel(
-    chunks, rec_in, src_in, cls_in, up, down, field, kinds, rec, src, cls, sems
+    chunks, rec_in, src_in, cls_in, inside, outside, field, kinds, rec, src, cls, sems
 ):
     fetch(((rec_in, rec), (src_in, src), (cls_in, cls)), sems)
+    lower = jnp.full((8, LANES), lax.axis_index("c"), jnp.int32) == 0
     for k in range(chunks):
         at = slice(k * LANES, (k + 1) * LANES)
         for p, (plane, part) in enumerate(((rec, 0), (rec, 1), (src, 0), (src, 1))):
             value = plane[part, 0, :, at]
             field[p, k] = value
-            up[k, 2 * p : 2 * p + 2, :] = value[6:8]
-            down[k, 2 * p : 2 * p + 2, :] = value[0:2]
+            inside[k, 2 * p : 2 * p + 2, :] = jnp.where(lower[0:2], value[6:8], value[0:2])
+            outside[k, 2 * p : 2 * p + 2, :] = jnp.where(lower[0:2], value[0:2], value[6:8])
         block, row = chunks + k // 8, k % 8
         index = cls[:, at]
         kinds[k] = index
-        up[block, row : row + 1, :] = index[7:8].astype(F32)
-        down[block, row : row + 1, :] = index[0:1].astype(F32)
+        top, bottom = index[0:1].astype(F32), index[7:8].astype(F32)
+        inside[block, row : row + 1, :] = jnp.where(lower[0:1], bottom, top)
+        outside[block, row : row + 1, :] = jnp.where(lower[0:1], top, bottom)
 
 
 def pick(table, index):
@@ -139,7 +137,7 @@
                 edge[6 + 3 * part + n, k] = pick(tap_rows(filt, t + 3), rim)
                 edge[12 + 3 * part + n, k] = pick(outward, next_rim)
 
-    each(chunks, load, 2)
+    each(chunks, load)
 
     def spread(k):
         for p in range(4):
@@ -169,18 +167,21 @@
                 field[p, k + 1] = parts[p]
 
     each(chunks, spread)
-    each(chunks, functools.partial(step, one, True), 2)
+    each(chunks, functools.partial(step, one, True))
     each(chunks, spread)
-    each(chunks, functools.partial(step, two, False), 2)
-
-
-def edge_kernel(chunks, place, filt, one, two, edge, up, down, above, below, out, rim, img):
+    each(chunks, functools.partial(step, two, False))
+
+
+def edge_kernel(
+    chunks, place, filt, one, two, edge, inside, outside, partner, other, out, rim, img
+):
     lane = lane_iota()
     row = row_iota()
     even = (row & 1) == 0
     pair = (row & 2) == 0
     flip = jnp.where((row < 2) | (row >= 6), -1.0, 1.0)
     zero = jnp.zeros((8, LANES), F32)
+    lower = jnp.full((8, LANES), place[6], jnp.int32) == 0
     low = jnp.where(place[0] == 0, 0.0, 1.0)
     high = jnp.where(place[0] == place[2] - 1, 0.0, 1.0)
     keep = jnp.where(even, low, high)
@@ -197,17 +198,19 @@
         return [(v, swap(v)) for v in (a, mid, b)]
 
     def load(k):
-        rim[0, k + 1] = jnp.where(even, above[k], up[k])
-        rim[1, k + 1] = jnp.where(even, pltpu.roll(above[k], 7, 0), pltpu.roll(below[k], 1, 0))
-        rim[2, k + 1] = jnp.where(even, down[k], below[k])
+        up, down = jnp.where(lower, inside[k], outside[k]), jnp.where(lower, outside[k], inside[k])
+        above, below = jnp.where(lower, other[k], partner[k]), jnp.where(lower, partner[k], other[k])
+        rim[0, k + 1] = jnp.where(even, above, up)
+        rim[1, k + 1] = jnp.where(even, pltpu.roll(above, 7, 0), pltpu.roll(below, 1, 0))
+        rim[2, k + 1] = jnp.where(even, down, below)
 
     each(chunks, load)
 
     def first(k):
         block = chunks + k // 8
-        over = above[block, pl.ds(k % 8, 1), :]
-        under = below[block, pl.ds(k % 8, 1), :]
-        index = jnp.where(even, over, under).astype(jnp.int32)
+        near_rows = partner[block, k % 8 : k % 8 + 1, :]
+        far_rows = other[block, k % 8 : k % 8 + 1, :]
+        index = jnp.where(even == lower, far_rows, near_rows).astype(jnp.int32)
         total = zero
         change = zero
         for m in range(3):
@@ -219,7 +222,7 @@
         rim[3, k + 1] = total * keep
         rim[4, k + 1] = change
 
-    each(chunks, first, 2)
+    each(chunks, first)
 
     def second(k):
         rows, nexts = zero, zero
@@ -243,7 +246,7 @@
         for d, (rr, ri, sr, si) in enumerate((ones, twos)):
             img[d, k + 1] = sr * rr + si * ri
 
-    each(chunks, second, 2)
+    each(chunks, second)
     for d in range(STEPS):
         img[d, 0] = zero
         img[d, chunks + 1] = zero
@@ -284,11 +287,11 @@
 
 
 def relay_kernel(place, near, energy, beside):
-    total = near[0, 2, 0:1, :]
+    total = near[0, 2]
     for n in range(1, near.shape[0]):
-        total = total + near[n, 2, 0:1, :]
+        total = total + near[n, 2]
     for n in range(energy.shape[0]):
-        energy[n] = total
+        energy[n] = total[0 : energy.shape[1]]
     start = place[3] * GROUP + jnp.where(place[4] < 4, 4, 0)
     for n in range(4):
         beside[n] = near[start + n]
@@ -318,14 +321,26 @@
     return jnp.where((lane < 32) | (lane >= 96), value + turned, turned - value)
 
 
-def table_kernel(place, index, spread, tables_out, mark, tables, sems):
-    kinds = spread.shape[1] // 2
+def strip_tables(place, index, points, s):
+    kinds = points.shape[1] // 2
     lane = lax.broadcasted_iota(jnp.int32, (2 * kinds, LANES), 1)
     kind = lax.broadcasted_iota(jnp.int32, (2 * kinds, LANES), 0)
     strips, groups = place[2], place[5]
     col = place[1]
     col_right = jnp.minimum(col + 1, groups - 1)
     col_left = jnp.maximum(col - 1, 0)
+    at = jnp.clip(place[0] + s - 4, 0, strips - 1)
+    own = index[at, col]
+    side = jnp.where((lane & 32) == 0, index[at, col_right], index[at, col_left])
+    side = jnp.where((lane < 32) | (lane >= 96), side, side + kinds)
+    chosen = [jnp.where(kind == v, 1.0, 0.0) for v in (own, own + kinds, side)]
+    return [
+        jnp.dot(points, v, precision=lax.Precision.HIGHEST, preferred_element_type=F32)
+        for v in chosen
+    ]
+
+
+def adjoint_kernel(place, index, spread, tables_out, mark, tables, sems):
     points = spread[...]
     mark[...] = jnp.zeros((8, LANES), F32)
     copies = []
@@ -336,19 +351,11 @@
         copies.append(copy)
 
     for s in range(9):
-        at = jnp.clip(place[0] + s - 4, 0, strips - 1)
-        own = index[at, col]
-        side = jnp.where((lane & 32) == 0, index[at, col_right], index[at, col_left])
-        side = jnp.where((lane < 32) | (lane >= 96), side, side + kinds)
-        chosen = [jnp.where(kind == v, 1.0, 0.0) for v in (own, own + kinds, side)]
-        values = [
-            jnp.dot(points, v, precision=lax.Precision.HIGHEST, preferred_element_type=F32)
-            for v in chosen
-        ]
-        if 2 <= s < 7:
+        values = strip_tables(place, index, points, s)
+        if s == 4:
             for q in range(3):
-                tables[7 + s, q] = values[q]
-            send(7 + s)
+                tables[9, q] = values[q]
+            send(9)
         for b in range(SIDE):
             rows = slice(16 * b, 16 * b + 16)
             turned = shifted(*(v[rows] for v in values), REACH - b)
@@ -359,12 +366,17 @@
         copy.wait()
 
 
-def table_copies(count, tables_in, tables, sems):
-    skip, inner = (9 - count) // 2, 9 + (9 - count) // 2
-    from_to = [(skip + n, n) for n in range(count)]
-    from_to += [(inner + n, count + n) for n in range(count - 4)]
-    for n, (a, b) in enumerate(from_to):
-        pltpu.make_async_copy(tables_in.at[a], tables.at[b], sems.at[n]).start()
+def forward_kernel(place, index, spread, after, tables):
+    points = spread[...]
+    for s in range(5):
+        values = strip_tables(place, index, points, s + 2)
+        for q in range(3):
+            tables[s, q] = values[q]
+
+
+def table_copies(which, tables_in, tables, sems):
+    for n, m in enumerate(which):
+        pltpu.make_async_copy(tables_in.at[m], tables.at[n], sems.at[n]).start()
 
     def ready(n):
         pltpu.make_async_copy(tables_in.at[0], tables.at[n], sems.at[n]).wait()
@@ -372,7 +384,9 @@
     return ready
 
 
-def operator_pass(count, place, resid, damping, tables, ready, rolled, acc, rolled_two, image):
+def operator_pass(
+    count, place, resid, damping, tables, ready, forward, first_table, rolled, acc, rolled_two, image
+):
     lane = lane_iota()
     row = row_iota()
     zero = jnp.zeros((8, LANES), F32)
@@ -391,21 +405,22 @@
         for s in range(count + 2):
             acc[q, 8 * s : 8 * s + 8, :] = zero
 
-    def back(s, carry):
+    def back(taps, s):
         base = pl.multiple_of(8 * s, 8)
         ready(s)
         for q in range(3):
             sums = [None] * SIDE
             for b in range(SIDE):
                 value = rolled[b, q, pl.ds(base, 8), :]
-                for a in range(SIDE):
+                for a in taps:
                     r = 16 * b + a
                     term = tables[s, q, r : r + 1, :] * value
                     sums[a] = term if sums[a] is None else sums[a] + term
-            lo, mid, hi = zero, sums[REACH], zero
-            for a in range(SIDE):
+            lo, mid, hi = zero, zero, zero
+            for a in taps:
                 m = a - REACH
                 if m == 0:
+                    mid = mid + sums[a]
                     continue
                 turned = pltpu.roll(sums[a], m % 8, 0)
                 if m > 0:
@@ -417,9 +432,19 @@
             for n, v in enumerate((lo, mid, hi)):
                 at = pl.ds(pl.multiple_of(base + 8 * n, 8), 8)
                 acc[q, at, :] = acc[q, at, :] + v
-        return carry
-
-    lax.fori_loop(0, count, back, 0)
+
+    for start, stop in ((0, 1), (1, count - 1), (count - 1, count)):
+        taps = range(SIDE)
+        if start == 0:
+            taps = range(REACH + 1, SIDE)
+        if stop == count:
+            taps = range(REACH)
+
+        def step(s, carry):
+            back(taps, s)
+            return carry
+
+        lax.fori_loop(start, stop, step, 0)
 
     halo_ok = jnp.where((lane & 32) == 0, place[1] + 1, place[5] - place[1]) < place[5]
     descent = None
@@ -435,26 +460,39 @@
             for q in range(3):
                 rolled_two[b, q, 8 * s - 8 : 8 * s, :] = turned[q]
 
-    def ahead(t, carry):
-        base = pl.multiple_of(8 * t, 8)
-        ready(count + t)
-        sums = [[None, None] for q in range(3)]
-        for a in range(SIDE):
-            for b in range(SIDE):
-                r = 16 * b + a
-                for q in range(3):
-                    term = tables[count + t, q, r : r + 1, :] * rolled_two[b, q, pl.ds(base + (a + 1), 8), :]
-                    n = b % 2
-                    sums[q][n] = term if sums[q][n] is None else sums[q][n] + term
+    def give(t, sums):
         at = place[0] + t - (count - 4) // 2
         row_ok = jnp.where((at >= 0) & (at < place[2]), 0.5, 0.0)
-        plus, minus, halo = ((v[0] + v[1]) * row_ok for v in sums)
+        plus, minus, halo = (v * row_ok for v in sums)
         image[t, 0] = plus + minus
         image[t, 1] = plus - minus
         image[t, 2] = jnp.where(halo_ok, halves(halo), 0.0)
-        return carry
-
-    lax.fori_loop(0, count - 4, ahead, 0)
+
+    def taps_of(rows, base):
+        for m in range(8):
+            for b in range(SIDE):
+                for q in range(3):
+                    value = rolled_two[b, q, pl.ds(base + (m + 1), 8), :]
+                    for t, low, sums in rows:
+                        a = m if low else m + 8
+                        if a < SIDE:
+                            r = 16 * b + a
+                            sums[q] = sums[q] + forward[first_table + t, q, r : r + 1, :] * value
+
+    if first_table:
+        ready(first_table)
+    sums = [zero] * 3
+    taps_of([(0, True, sums)], 0)
+
+    def ahead(t, carry):
+        old, new = list(carry), [zero] * 3
+        taps_of([(t - 1, False, old), (t, True, new)], pl.multiple_of(8 * t, 8))
+        give(t - 1, old)
+        return tuple(new)
+
+    sums = list(lax.fori_loop(1, count - 4, ahead, tuple(sums)))
+    taps_of([(count - 5, False, sums)], 8 * (count - 4))
+    give(count - 5, sums)
     plus, minus = descent
     return 0.5 * (plus + minus), 0.5 * (plus - minus)
 
@@ -475,10 +513,10 @@
 
 
 def gathered(parts):
-    total = parts[0]
-    for n in range(1, parts.shape[0]):
-        total = total + parts[n]
-    return total
+    sums = [parts[n, 0:1] for n in range(4)]
+    for n in range(4, parts.shape[0]):
+        sums[n % 4] = sums[n % 4] + parts[n, 0:1]
+    return (sums[0] + sums[1]) + (sums[2] + sums[3])
 
 
 def at_lane(total, spot):
@@ -487,10 +525,10 @@
 
 
 def first_kernel(
-    place, energies, near, beside, tables_in, payload, state, descent, energy,
-    strips, resid, image, tables, sems, rolled, acc, rolled_two,
+    place, energies, near, beside, forward, tables_in, payload, state, descent, energy,
+    strips, tables, sems, resid, image, rolled, acc, rolled_two,
 ):
-    ready = table_copies(9, tables_in, tables, sems)
+    ready = table_copies(range(9), tables_in, tables, sems)
     total = at_lane(gathered(energies), ENERGY_LANE)
     energy[...] = jnp.broadcast_to(total, (1, LANES))
     damping = total / CELLS
@@ -503,7 +541,9 @@
     start = lax.rem(place[4], 4)
     for s in range(9):
         resid[s] = strips[start + s]
-    pair = operator_pass(9, place, resid, damping, tables, ready, rolled, acc, rolled_two, image)
+    pair = operator_pass(
+        9, place, resid, damping, tables, ready, forward, 0, rolled, acc, rolled_two, image
+    )
     for d in range(STEPS):
         descent[d] = pair[d]
     for s in range(5):
@@ -523,9 +563,9 @@
 
 def second_kernel(
     place, parts, energy, state, descent_in, tables_in, payload, descent, model,
-    resid, image, tables, sems, rolled, acc, rolled_two,
+    tables, sems, resid, image, rolled, acc, rolled_two,
 ):
-    ready = table_copies(5, tables_in, tables, sems)
+    ready = table_copies((2, 3, 4, 5, 6, 9), tables_in, tables, sems)
     step, after = step_and_energy(parts, energy[:, 0:1])
     damping = after / CELLS
     for s in range(5):
@@ -533,7 +573,10 @@
             resid[s, d] = state[s, d] - step * state[5 + s, d]
     for d in range(STEPS):
         model[d] = -(step * descent_in[d])
-    pair = operator_pass(5, place, resid, damping, tables, ready, rolled, acc, rolled_two, image)
+
+    pair = operator_pass(
+        5, place, resid, damping, tables, ready, tables, 5, rolled, acc, rolled_two, image
+    )
     for d in range(STEPS):
         descent[d] = pair[d]
     five_sums(pair, resid, image, 2, damping, payload)
@@ -567,7 +610,7 @@
     group = lax.axis_index(FREQ)
     half = lax.axis_index("yh")
     place = jnp.stack(
-        [strip, group, jnp.int32(strips), half, lax.rem(strip, GROUP), jnp.int32(groups)]
+        [strip, group, jnp.int32(strips), half, lax.rem(strip, GROUP), jnp.int32(groups), lax.axis_index("c")]
     ).astype(jnp.int32)
 
     blocks = chunks + chunks // 8
@@ -576,7 +619,7 @@
         pltpu.VMEM(source_field.shape, F32),
         pltpu.VMEM(velocity_class.shape, jnp.int32),
     ]
-    up, down, given, kinds = pl.pallas_call(
+    inside, outside, given, kinds = pl.pallas_call(
         functools.partial(pack_kernel, chunks),
         out_shape=(
             shape(blocks, 8, LANES),
@@ -587,23 +630,25 @@
         in_specs=[HBM] * 3,
         out_specs=tuple(whole(4)),
         scratch_shapes=landing + [pltpu.SemaphoreType.DMA((3,))],
-        compiler_params=params(16),
+        compiler_params=params(),
         name="pack",
     )(receiver_field, source_field, velocity_class)
-    above = lax.ppermute(up, STRIP, [(i, i + 1) for i in range(strips - 1)])
-    below = lax.ppermute(down, STRIP, [(i + 1, i) for i in range(strips - 1)])
+    swaps = [(i, i ^ 1) for i in range(strips)]
+    partner = lax.ppermute(inside, STRIP, swaps)
+    crossings = [(i, i - 1 if i % 2 == 0 else i + 1) for i in range(1, strips - 1)]
+    other = lax.ppermute(outside, STRIP, crossings)
 
     points = jnp.concatenate(
         [point_spread[:, 0] + point_spread[:, 1], point_spread[:, 0] - point_spread[:, 1]]
     ).transpose(2, 1, 0)
     points = jnp.pad(points, ((0, 0), (0, 1), (0, 0))).reshape(TAPS, -1)
     tables, mark = pl.pallas_call(
-        table_kernel,
-        out_shape=(shape(14, 3, TAPS, LANES), shape(8, LANES)),
+        adjoint_kernel,
+        out_shape=(shape(24, 3, TAPS, LANES), shape(8, LANES)),
         in_specs=[SMEM, SMEM] + whole(1),
         out_specs=(HBM, whole(1)[0]),
-        scratch_shapes=[pltpu.VMEM((14, 3, TAPS, LANES), F32), pltpu.SemaphoreType.DMA((14,))],
-        compiler_params=params(52),
+        scratch_shapes=[pltpu.VMEM((10, 3, TAPS, LANES), F32), pltpu.SemaphoreType.DMA((10,))],
+        compiler_params=params(47),
         cost_estimate=pl.CostEstimate(flops=100000000, bytes_accessed=8000000, transcendentals=0),
         name="tables",
     )(place, spread_index, points)
@@ -641,7 +686,7 @@
         ],
         compiler_params=params(),
         name="edges",
-    )(place, filt, one, two, edge, up, down, above, below)
+    )(place, filt, one, two, edge, inside, outside, partner, other)
     terms = lax.all_to_all(terms, FREQ, 0, 0)
 
     nearby = SHAPE[1] * SHAPE[3] * SHAPE[4]
@@ -657,26 +702,33 @@
     near = lax.all_to_all(payload, NEAR, 0, 0)
     energies, beside = pl.pallas_call(
         relay_kernel,
-        out_shape=(shape(far, 1, LANES), shape(4, 3, 8, LANES)),
+        out_shape=(shape(far, 2, LANES), shape(4, 3, 8, LANES)),
         in_specs=[SMEM] + whole(1),
         out_specs=tuple(whole(2)),
         compiler_params=params(),
         name="relay",
     )(place, near)
+    exchanged = lax.all_to_all(energies, FAR, 0, 0)
     pairs = []
     for i in range(strips):
         to = i + GROUP if i % GROUP < 4 else i - GROUP
         if 0 <= to < strips:
             pairs.append((i, to))
     beside = lax.ppermute(beside, STRIP, pairs)
-    energies = lax.all_to_all(energies, FAR, 0, 0)
+    forward = pl.pallas_call(
+        forward_kernel,
+        out_shape=shape(5, 3, TAPS, LANES),
+        in_specs=[SMEM, SMEM] + whole(2),
+        out_specs=whole(1)[0],
+        compiler_params=params(),
+        cost_estimate=pl.CostEstimate(flops=100000000, bytes_accessed=8000000, transcendentals=0),
+        name="ahead",
+    )(place, spread_index, points, energies)
 
     def scratch(count):
         return [
             pltpu.VMEM((count, 3, 8, LANES), F32),
             pltpu.VMEM((count - 4, 3, 8, LANES), F32),
-            pltpu.VMEM((2 * count - 4, 3, TAPS, LANES), F32),
-            pltpu.SemaphoreType.DMA((2 * count - 4,)),
             pltpu.VMEM((SIDE, 3, 8 * count, LANES), F32),
             pltpu.VMEM((3, 8 * count + 16, LANES), F32),
             pltpu.VMEM((SIDE, 3, 8 * count - 16, LANES), F32),
@@ -690,20 +742,26 @@
             shape(STEPS, 8, LANES),
             shape(1, LANES),
         ),
-        in_specs=[SMEM] + whole(3) + [HBM],
+        in_specs=[SMEM] + whole(4) + [HBM],
         out_specs=tuple(whole(4)),
-        scratch_shapes=[pltpu.VMEM((12, 3, 8, LANES), F32)] + scratch(9),
-        compiler_params=params(52),
+        scratch_shapes=[
+            pltpu.VMEM((12, 3, 8, LANES), F32),
+            pltpu.VMEM((9, 3, TAPS, LANES), F32),
+            pltpu.SemaphoreType.DMA((9,)),
+        ]
+        + scratch(9),
+        compiler_params=params(47),
         name="pass_one",
-    )(place, energies, near, beside, tables)
+    )(place, exchanged, near, beside, forward, tables)
     parts = all_sum(parts)
     parts, descent, model = pl.pallas_call(
         second_kernel,
         out_shape=(shape(nearby, 1, LANES), shape(STEPS, 8, LANES), shape(STEPS, 8, LANES)),
         in_specs=[SMEM] + whole(4) + [HBM],
         out_specs=tuple(whole(3)),
-        scratch_shapes=scratch(5),
-        compiler_params=params(52),
+        scratch_shapes=[pltpu.VMEM((6, 3, TAPS, LANES), F32), pltpu.SemaphoreType.DMA((6,))]
+        + scratch(5),
+        compiler_params=params(47),
         name="pass_two",
     )(place, parts, energy, state, descent, tables)
     parts = all_sum(parts)

time: 142 us -> 136 us (0.958)
  blocking collectives: 78.3 us -> 64 us
  starting transfers between devices: 24.9 us -> 30.9 us
  waiting for transfers between devices: 5.7 us -> 10.8 us
  local copies, waits for them, and re-layouts: 6 us -> 4.24 us
    all_to_all x1 -> x0, blocking collectives: 15.7 us -> none  [local(): energies = lax.all_to_all(energies, FAR, 0, 0)]
    all_to_all x0 -> x1, starting transfers between devices: none -> 6.99 us  [local(): exchanged = lax.all_to_all(energies, FAR, 0, 0)]
    all_to_all x0 -> x1, waiting for transfers between devices: none -> 3.15 us  [local(): exchanged = lax.all_to_all(energies, FAR, 0, 0)]
    pallas_call x2 -> x3, Pallas kernels: 5.12 us -> 8.07 us  [the longest x1 4.52 us: local(): pl.pallas_call(adjoint_kernel, out_shape=(shape(24, 3, TAPS, LANES), shap...]
    all_to_all x2, blocking collectives: 23.1 us -> 25.6 us  [all_sum(): lax.all_to_all(jnp.broadcast_to(total[None], (ways, 1, LANES)), FAR, 0, 0)]
    pallas_call x1, Pallas kernels: 3.63 us -> 2.03 us  [local(): pl.pallas_call(functools.partial(inner_kernel, chunks), out_shape=(shape(...]
    unnamed x12 -> x16, local copies, waits for them, and re-layouts: 4.61 us -> 3.92 us
  transfers between devices with their start and end apart: 4 -> 5, of which waited for: 1 -> 3; matrix products, arithmetic and copies ran while one was open for 2% -> 1% of each run, Pallas kernels for 6% -> 7%
where the time goes in v3:
time: 136 us; the launch traced here: 135 us
  blocking collectives  64 us (47%)
  starting transfers between devices  30.9 us (23%)
  Pallas kernels  24.4 us (18%)
  waiting for transfers between devices  10.8 us (8%)
  local copies, waits for them, and re-layouts  4.24 us (3%)
    all_to_all x2, blocking collectives, all_sum(): lax.all_to_all(jnp.broadcast_to(total[None], (ways, 1, LANES)), FAR, 0, 0)  25.6 us
    all_to_all x2, blocking collectives, all_sum(): near = lax.all_to_all(parts, NEAR, 0, 0)  22.6 us
    all_to_all x1, blocking collectives, local(): near = lax.all_to_all(payload, NEAR, 0, 0)  15.7 us
    all_to_all x1, starting transfers between devices, local(): terms = lax.all_to_all(terms, FREQ, 0, 0)  10 us
    ppermute x1, starting transfers between devices, local(): partner = lax.ppermute(inside, STRIP, swaps)  8.79 us
    all_to_all x1, starting transfers between devices, local(): exchanged = lax.all_to_all(energies, FAR, 0, 0)  6.99 us
    pallas_call x1, Pallas kernels, local(): pl.pallas_call(first_kernel, out_shape=(shape(nearby, 1, LANES), shape(10...  6.75 us
    all_to_all x1, waiting for transfers between devices, local(): terms = lax.all_to_all(terms, FREQ, 0, 0)  6.72 us
  transfers between devices with their start and end apart: 5, of which 3 were waited for; matrix products, arithmetic and copies ran while one was open for 1% of the time, Pallas kernels for 7%

profile of v3, /device:TPU:1, one launch (start us, length us, event | category | flops | bytes accessed | tf_op | source)
XLA Modules:
  0.0 135.2 jit_solution(2044137534870800349)
XLA Ops:
  0.6 0.0 copy-start
  0.6 0.9 copy-done
  1.5 0.0 copy-start.1
  1.5 0.9 copy-done.1
  2.4 0.0 copy-start.2
  2.4 0.8 copy-done.2
  3.3 0.0 copy-start.4
  3.3 0.0 copy-start.5
  3.3 0.5 pack.1
  3.8 8.8 %collective-permute-start = (f32[18,8,128]{2,1,0:T(8,128)S(1)}, f32[18,8,128]{2,1,0:T(8,128)S(1)}, u32[]{:S(2)}, u32[]{:S(2)}) collective-permute-start(f32[18,8,128]{2,1,0:T(8,128)S(1)} %get-tuple-element.32.inside), channel_id=1, source_target_pairs={{0,1},{1,0},{2,3},{3,2},{4,5},{5,4},{6,7},{7,6},{8,9},{9,8},{10,11... | collective-permute-start | bytes 221192 | tf_op jit(solution)/shard_map/ppermute | solution.py:637
  12.6 1.9 %collective-permute-start.1 = (f32[18,8,128]{2,1,0:T(8,128)S(1)}, f32[18,8,128]{2,1,0:T(8,128)S(1)}, u32[]{:S(2)}, u32[]{:S(2)}) collective-permute-start(f32[18,8,128]{2,1,0:T(8,128)S(1)} %get-tuple-element.33.outside), channel_id=1, source_target_pairs={{1,2},{2,1},{3,4},{4,3},{5,6},{6,5},{7,8},{8,7},{9,10},{10,9},{11,... | collective-permute-start | bytes 221192 | tf_op jit(solution)/shard_map/ppermute | solution.py:639
  14.5 0.1 stack.24.place
  14.6 0.0 copy-start.3
  14.6 0.7 copy-done.3
  15.3 2.0 %inner.1 = (f32[4,16,8,128]{3,2,1,0:T(8,128)S(1)}, f32[4,16,8,128]{3,2,1,0:T(8,128)S(1)}, f32[18,16,8,128]{3,2,1,0:T(8,128)S(1)}, f32[18,128]{1,0:T(8,128)S(1)}) custom-call(f32[4,16,8,128]{3,2,1,0:T(8,128)S(1)} %get-tuple-element.26.given, s32[16,8,128]{2,1,0:T(8,128)S(1)} %get-tuple-element.27.kinds, f32[1,8,2,9]{3,2,1,0:T(2,128)S(1)} %copy-done.3), custom_call_target="tpu_custom_call" | custom-call | flops 100000000 | bytes 8000000 | tf_op jit(solution)/shard_map/inner/pallas_call | solution.py:657
  17.3 0.0 collective-permute-done.partner
  17.4 0.9 collective-permute-done.1.other
  18.3 2.1 %edges.1 = f32[16,3,8,128]{3,2,1,0:T(8,128)} custom-call(s32[7]{0:T(128)S(1)} %stack.24.place, f32[18,128]{1,0:T(8,128)S(1)} %get-tuple-element.28.filt, f32[4,16,8,128]{3,2,1,0:T(8,128)S(1)} %get-tuple-element.29.one, f32[4,16,8,128]{3,2,1,0:T(8,128)S(1)} %get-tuple-element.30.two, f32[18,16,8,128]{3,2,1,0:T(8,128)S(1)} %get-tuple-element.31.edge, ...), custom_call_target="tpu_custom_call" | custom-call | tf_op jit(solution)/shard_map/edges/pallas_call | solution.py:678
  20.4 10.0 %all-to-all-start = ((f32[16,3,8,128]{3,2,1,0:T(8,128)}), f32[16,3,8,128]{3,2,1,0:T(8,128)S(1)}, u32[]{:S(2)}, u32[]{:S(2)}) async-start(f32[16,3,8,128]{3,2,1,0:T(8,128)} %edges.1), calls=%async_computation | async-start | bytes 393216 | tf_op jit(solution)/shard_map/all_to_all | solution.py:690
  30.4 0.0 copy-done.4
  30.4 0.2 fusion
  30.6 0.0 copy-done.5
  30.6 0.1 copy.18.index
  30.7 0.2 copy.21
  30.9 0.2 copy.20
  31.1 0.2 copy.22
  31.3 4.5 %tables.1 = (f32[24,3,240,128]{3,2,1,0:T(8,128)}, f32[8,128]{1,0:T(8,128)S(1)}) custom-call(s32[7]{0:T(128)S(1)} %stack.24.place, s32[32,16]{1,0:T(8,128)S(1)} %copy.18.index, f32[240,32]{1,0:T(8,128)S(1)} %bitcast.13), custom_call_target="tpu_custom_call" | custom-call | flops 100000000 | bytes 8000000 | tf_op jit(solution)/shard_map/tables/pallas_call | solution.py:645
  35.8 6.7 %all-to-all-done.terms = f32[16,3,8,128]{3,2,1,0:T(8,128)S(1)} async-done(((f32[16,3,8,128]{3,2,1,0:T(8,128)}), f32[16,3,8,128]{3,2,1,0:T(8,128)S(1)}, u32[]{:S(2)}, u32[]{:S(2)}) %all-to-all-start) | async-done | bytes 196640 | tf_op jit(solution)/shard_map/all_to_all | solution.py:690
  42.6 0.6 stack.25
  43.2 15.7 %all_to_all.35.near = f32[16,3,8,128]{3,2,1,0:T(8,128)S(1)} all-to-all(f32[16,3,8,128]{3,2,1,0:T(8,128)S(1)} %get-tuple-element.36), channel_id=1, replica_groups=mesh['z'=8,'yh'=2,'x'=4,'yl'=4,'c'=2] {'yh','yl','c'}, dimensions={0} | all-to-all | bytes 393216 | tf_op jit(solution)/shard_map/all_to_all | solution.py:702
  58.9 1.2 relay.1
  60.1 7.0 %all-to-all-start.2 = ((f32[32,2,128]{2,1,0:T(2,128)}), f32[32,2,128]{2,1,0:T(2,128)S(1)}, u32[]{:S(2)}, u32[]{:S(2)}) async-start(f32[32,2,128]{2,1,0:T(2,128)} %get-tuple-element.37.after), calls=%async_computation.2 | async-start | bytes 65536 | tf_op jit(solution)/shard_map/all_to_all | solution.py:711
  67.1 3.1 %collective-permute-start.2 = (f32[4,3,8,128]{3,2,1,0:T(8,128)S(1)}, f32[4,3,8,128]{3,2,1,0:T(8,128)S(1)}, u32[]{:S(2)}, u32[]{:S(2)}) collective-permute-start(f32[4,3,8,128]{3,2,1,0:T(8,128)S(1)} %get-tuple-element.38), channel_id=1, source_target_pairs={{0,8},{1,9},{2,10},{3,11},{8,16},{9,17},{10,18},{11,19},{12,4},{13... | collective-permute-start | bytes 147464 | tf_op jit(solution)/shard_map/ppermute | solution.py:717
  70.2 2.4 %ahead.1.forward = f32[5,3,240,128]{3,2,1,0:T(8,128)S(1)} custom-call(s32[7]{0:T(128)S(1)} %stack.24.place, s32[32,16]{1,0:T(8,128)S(1)} %copy.18.index, f32[240,32]{1,0:T(8,128)S(1)} %bitcast.14, f32[32,2,128]{2,1,0:T(2,128)} %get-tuple-element.37.after), custom_call_target="tpu_custom_call" | custom-call | flops 100000000 | bytes 8000000 | tf_op jit(solution)/shard_map/ahead/pallas_call | solution.py:718
  72.6 0.0 collective-permute-done.2.beside
  72.6 3.1 %all-to-all-done.2.energies = f32[32,2,128]{2,1,0:T(2,128)S(1)} async-done(((f32[32,2,128]{2,1,0:T(2,128)}), f32[32,2,128]{2,1,0:T(2,128)S(1)}, u32[]{:S(2)}, u32[]{:S(2)}) %all-to-all-start.2) | async-done | bytes 32800 | tf_op jit(solution)/shard_map/all_to_all | solution.py:711
  75.8 6.7 %pass_one.1 = (f32[16,1,128]{2,1,0:T(1,128)S(1)}, f32[10,3,8,128]{3,2,1,0:T(8,128)S(1)}, f32[2,8,128]{2,1,0:T(8,128)S(1)}, f32[1,128]{1,0:T(1,128)S(1)}) custom-call(s32[7]{0:T(128)S(1)} %stack.24.place, f32[32,2,128]{2,1,0:T(2,128)S(1)} %all-to-all-done.2.energies, f32[16,3,8,128]{3,2,1,0:T(8,128)S(1)} %all_to_all.35.near, ...), custom_call_target="tpu_custom_call" | custom-call | tf_op jit(solution)/shard_map/pass_one/pallas_call | solution.py:737
  82.5 11.1 %all_to_all.36 = f32[16,1,128]{2,1,0:T(1,128)S(1)} all-to-all(f32[16,1,128]{2,1,0:T(1,128)S(1)} %get-tuple-element.40), channel_id=1, replica_groups=mesh['z'=8,'yh'=2,'x'=4,'yl'=4,'c'=2] {'yh','yl','c'}, dimensions={0} | all-to-all | bytes 16384 | tf_op jit(solution)/shard_map/all_to_all | solution.py:597
  93.6 14.1 %all_to_all.37.parts = f32[32,1,128]{2,1,0:T(1,128)S(1)} all-to-all(f32[32,1,128]{2,1,0:T(1,128)S(1)} %broadcast_in_dim.4), channel_id=1, replica_groups=mesh['z'=8,'yh'=2,'x'=4,'yl'=4,'c'=2] {'z','x'}, dimensions={0} | all-to-all | bytes 32768 | tf_op jit(solution)/shard_map/all_to_all | solution.py:600
  107.7 3.6 %pass_two.1 = (f32[16,1,128]{2,1,0:T(1,128)S(1)}, f32[2,8,128]{2,1,0:T(8,128)S(1)}, f32[2,8,128]{2,1,0:T(8,128)S(1)}) custom-call(s32[7]{0:T(128)S(1)} %stack.24.place, f32[32,1,128]{2,1,0:T(1,128)S(1)} %all_to_all.37.parts, f32[1,128]{1,0:T(1,128)S(1)} %get-tuple-element.41.energy, f32[10,3,8,128]{3,2,1,0:T(8,128)S(1)} %get-tuple-element.42.state, ...), custom_call_target="tpu_custom_call" | custom-call | tf_op jit(solution)/shard_map/pass_two/pallas_call | solution.py:757
  111.3 11.5 %all_to_all.38 = f32[16,1,128]{2,1,0:T(1,128)S(1)} all-to-all(f32[16,1,128]{2,1,0:T(1,128)S(1)} %get-tuple-element.44), channel_id=1, replica_groups=mesh['z'=8,'yh'=2,'x'=4,'yl'=4,'c'=2] {'yh','yl','c'}, dimensions={0} | all-to-all | bytes 16384 | tf_op jit(solution)/shard_map/all_to_all | solution.py:597
  122.9 11.6 %all_to_all.39.parts = f32[32,1,128]{2,1,0:T(1,128)S(1)} all-to-all(f32[32,1,128]{2,1,0:T(1,128)S(1)} %broadcast_in_dim.5), channel_id=1, replica_groups=mesh['z'=8,'yh'=2,'x'=4,'yl'=4,'c'=2] {'z','x'}, dimensions={0} | all-to-all | bytes 32768 | tf_op jit(solution)/shard_map/all_to_all | solution.py:600
  134.4 0.7 last.1
  (7 shorter events, 0.2 us)
Async XLA Ops:
  0.6 0.9 copy-start
  1.5 0.9 copy-start.1
  2.4 0.8 copy-start.2
  3.3 27.2 %copy-start.4 = (f32[16,2,15,15]{0,1,3,2:T(2,128)S(1)}, f32[16,2,15,15]{0,1,3,2:T(2,128)}, u32[]{:S(2)}) copy-start(f32[16,2,15,15]{0,1,3,2:T(2,128)} %param.10) | copy-start | bytes 86404
  3.3 27.4 %copy-start.5 = (s32[32,16]{0,1:T(8,128)S(1)}, s32[32,16]{0,1:T(8,128)}, u32[]{:S(2)}) copy-start(s32[32,16]{0,1:T(8,128)} %param.11) | copy-start | bytes 6148
  3.8 13.6 %collective-permute-start = (f32[18,8,128]{2,1,0:T(8,128)S(1)}, f32[18,8,128]{2,1,0:T(8,128)S(1)}, u32[]{:S(2)}, u32[]{:S(2)}) collective-permute-start(f32[18,8,128]{2,1,0:T(8,128)S(1)} %get-tuple-element.32.inside), channel_id=1, source_target_pairs={{0,1},{1,0},{2,3},{3,2},{4,5},{5,4},{6,7},{7,6},{8,9},{9,8},{10,11... | collective-permute-start | bytes 221192 | tf_op jit(solution)/shard_map/ppermute | solution.py:637
  12.6 5.7 %collective-permute-start.1 = (f32[18,8,128]{2,1,0:T(8,128)S(1)}, f32[18,8,128]{2,1,0:T(8,128)S(1)}, u32[]{:S(2)}, u32[]{:S(2)}) collective-permute-start(f32[18,8,128]{2,1,0:T(8,128)S(1)} %get-tuple-element.33.outside), channel_id=1, source_target_pairs={{1,2},{2,1},{3,4},{4,3},{5,6},{6,5},{7,8},{8,7},{9,10},{10,9},{11,... | collective-permute-start | bytes 221192 | tf_op jit(solution)/shard_map/ppermute | solution.py:639
  14.6 0.7 copy-start.3
  20.4 22.2 %all-to-all-start = ((f32[16,3,8,128]{3,2,1,0:T(8,128)}), f32[16,3,8,128]{3,2,1,0:T(8,128)S(1)}, u32[]{:S(2)}, u32[]{:S(2)}) async-start(f32[16,3,8,128]{3,2,1,0:T(8,128)} %edges.1), calls=%async_computation | async-start | bytes 393216 | tf_op jit(solution)/shard_map/all_to_all | solution.py:690
  60.1 15.7 %all-to-all-start.2 = ((f32[32,2,128]{2,1,0:T(2,128)}), f32[32,2,128]{2,1,0:T(2,128)S(1)}, u32[]{:S(2)}, u32[]{:S(2)}) async-start(f32[32,2,128]{2,1,0:T(2,128)} %get-tuple-element.37.after), calls=%async_computation.2 | async-start | bytes 65536 | tf_op jit(solution)/shard_map/all_to_all | solution.py:711
  67.1 5.5 %collective-permute-start.2 = (f32[4,3,8,128]{3,2,1,0:T(8,128)S(1)}, f32[4,3,8,128]{3,2,1,0:T(8,128)S(1)}, u32[]{:S(2)}, u32[]{:S(2)}) collective-permute-start(f32[4,3,8,128]{3,2,1,0:T(8,128)S(1)} %get-tuple-element.38), channel_id=1, source_target_pairs={{0,8},{1,9},{2,10},{3,11},{8,16},{9,17},{10,18},{11,19},{12,4},{13... | collective-permute-start | bytes 147464 | tf_op jit(solution)/shard_map/ppermute | solution.py:717

commit v4 on v3

--- a/solution.py
+++ b/solution.py
@@ -45,6 +45,13 @@
 
 def row_iota():
     return lax.broadcasted_iota(jnp.int32, (8, LANES), 0)
+
+
+def whereabouts():
+    z, yh, x, yl, c = (lax.axis_index(name) for name in NAMES)
+    spot = yl * SHAPE[4] + c
+    strips, groups = SHAPE[2] * SHAPE[3] * SHAPE[4], SHAPE[0] * SHAPE[1]
+    return x * GROUP + spot, z * SHAPE[1] + yh, strips, yh, spot, groups, c
 
 
 def each(count, step):
@@ -173,8 +180,9 @@
 
 
 def edge_kernel(
-    chunks, place, filt, one, two, edge, inside, outside, partner, other, out, rim, img
+    chunks, filt, one, two, edge, inside, outside, partner, other, out, rim, img
 ):
+    place = whereabouts()
     lane = lane_iota()
     row = row_iota()
     even = (row & 1) == 0
@@ -286,7 +294,8 @@
         payload[n, 2] = halo
 
 
-def relay_kernel(place, near, energy, beside):
+def relay_kernel(near, energy, beside):
+    place = whereabouts()
     total = near[0, 2]
     for n in range(1, near.shape[0]):
         total = total + near[n, 2]
@@ -322,7 +331,7 @@
 
 
 def strip_tables(place, index, points, s):
-    kinds = points.shape[1] // 2
+    kinds = points[0].shape[1] // 2
     lane = lax.broadcasted_iota(jnp.int32, (2 * kinds, LANES), 1)
     kind = lax.broadcasted_iota(jnp.int32, (2 * kinds, LANES), 0)
     strips, groups = place[2], place[5]
@@ -333,15 +342,24 @@
     own = index[at, col]
     side = jnp.where((lane & 32) == 0, index[at, col_right], index[at, col_left])
     side = jnp.where((lane < 32) | (lane >= 96), side, side + kinds)
-    chosen = [jnp.where(kind == v, 1.0, 0.0) for v in (own, own + kinds, side)]
-    return [
-        jnp.dot(points, v, precision=lax.Precision.HIGHEST, preferred_element_type=F32)
-        for v in chosen
-    ]
-
-
-def adjoint_kernel(place, index, spread, tables_out, mark, tables, sems):
-    points = spread[...]
+    chosen = jnp.concatenate(
+        [jnp.where(kind == v, 1.0, 0.0) for v in (own, own + kinds, side)], axis=1
+    ).astype(jnp.bfloat16)
+    parts = [jnp.dot(v, chosen, preferred_element_type=F32) for v in points]
+    value = (parts[0] + parts[1]) + parts[2]
+    return [value[:, q * LANES : (q + 1) * LANES] for q in range(3)]
+
+
+def three_parts(value):
+    high = value.astype(jnp.bfloat16)
+    rest = value - high.astype(F32)
+    middle = rest.astype(jnp.bfloat16)
+    return high, middle, (rest - middle.astype(F32)).astype(jnp.bfloat16)
+
+
+def adjoint_kernel(index, spread, tables_out, mark, tables, sems):
+    place = whereabouts()
+    points = three_parts(spread[...])
     mark[...] = jnp.zeros((8, LANES), F32)
     copies = []
 
@@ -366,8 +384,9 @@
         copy.wait()
 
 
-def forward_kernel(place, index, spread, after, tables):
-    points = spread[...]
+def forward_kernel(index, spread, after, tables):
+    place = whereabouts()
+    points = three_parts(spread[...])
     for s in range(5):
         values = strip_tables(place, index, points, s + 2)
         for q in range(3):
@@ -498,16 +517,20 @@
 
 
 def five_sums(descent, resid, image, middle, damping, payload):
-    lane = lax.broadcasted_iota(jnp.int32, (1, LANES), 1)
     sums = [jnp.zeros((8, LANES), F32)] * 5
     for d in range(STEPS):
         g, r, q = descent[d], resid[middle, d], image[middle - 2, d]
         w = 1.0 / jnp.sqrt(r * r + damping)
         for n, v in enumerate((g * g, w * q * q, r * q, q * q, r * r)):
             sums[n] = sums[n] + v
-    value = jnp.zeros((1, LANES), F32)
+    row = row_iota()
+    packed = jnp.zeros((8, LANES), F32)
     for n in range(5):
-        value = jnp.where((lane >= 16 * n) & (lane < 16 * n + 16), total_of(sums[n]), value)
+        packed = jnp.where(row == n, jnp.sum(sums[n], axis=0, keepdims=True), packed)
+    packed = jnp.sum(packed, axis=1, keepdims=True)
+    lane = lane_iota()
+    value = jnp.where((row == lane // 16) & (lane < 80), packed, 0.0)
+    value = jnp.sum(value, axis=0, keepdims=True)
     for n in range(payload.shape[0]):
         payload[n] = value
 
@@ -520,15 +543,15 @@
 
 
 def at_lane(total, spot):
-    lane = lax.broadcasted_iota(jnp.int32, (1, LANES), 1)
-    return jnp.sum(jnp.where(lane == spot, total, 0.0), axis=1, keepdims=True)
+    return total[:, spot : spot + 1]
 
 
 def first_kernel(
-    place, energies, near, beside, forward, tables_in, payload, state, descent, energy,
+    energies, near, beside, forward, tables_in, payload, state, descent, energy,
     strips, tables, sems, resid, image, rolled, acc, rolled_two,
 ):
     ready = table_copies(range(9), tables_in, tables, sems)
+    place = whereabouts()
     total = at_lane(gathered(energies), ENERGY_LANE)
     energy[...] = jnp.broadcast_to(total, (1, LANES))
     damping = total / CELLS
@@ -562,10 +585,11 @@
 
 
 def second_kernel(
-    place, parts, energy, state, descent_in, tables_in, payload, descent, model,
+    parts, energy, state, descent_in, tables_in, payload, descent, model,
     tables, sems, resid, image, rolled, acc, rolled_two,
 ):
     ready = table_copies((2, 3, 4, 5, 6, 9), tables_in, tables, sems)
+    place = whereabouts()
     step, after = step_and_energy(parts, energy[:, 0:1])
     damping = after / CELLS
     for s in range(5):
@@ -606,13 +630,6 @@
     columns = velocity_class.shape[1]
     chunks = columns // LANES
     scaling = 1.0 / math.sqrt(groups)
-    strip = lax.axis_index(STRIP)
-    group = lax.axis_index(FREQ)
-    half = lax.axis_index("yh")
-    place = jnp.stack(
-        [strip, group, jnp.int32(strips), half, lax.rem(strip, GROUP), jnp.int32(groups), lax.axis_index("c")]
-    ).astype(jnp.int32)
-
     blocks = chunks + chunks // 8
     landing = [
         pltpu.VMEM(receiver_field.shape, F32),
@@ -645,13 +662,13 @@
     tables, mark = pl.pallas_call(
         adjoint_kernel,
         out_shape=(shape(24, 3, TAPS, LANES), shape(8, LANES)),
-        in_specs=[SMEM, SMEM] + whole(1),
+        in_specs=[SMEM] + whole(1),
         out_specs=(HBM, whole(1)[0]),
         scratch_shapes=[pltpu.VMEM((10, 3, TAPS, LANES), F32), pltpu.SemaphoreType.DMA((10,))],
         compiler_params=params(47),
         cost_estimate=pl.CostEstimate(flops=100000000, bytes_accessed=8000000, transcendentals=0),
         name="tables",
-    )(place, spread_index, points)
+    )(spread_index, points)
 
     planes = chunks + 2
     one, two, edge, filt = pl.pallas_call(
@@ -678,7 +695,7 @@
     terms = pl.pallas_call(
         functools.partial(edge_kernel, chunks),
         out_shape=shape(chunks, 3, 8, LANES),
-        in_specs=[SMEM] + whole(8),
+        in_specs=whole(8),
         out_specs=whole(1)[0],
         scratch_shapes=[
             pltpu.VMEM((5, planes, 8, LANES), F32),
@@ -686,7 +703,7 @@
         ],
         compiler_params=params(),
         name="edges",
-    )(place, filt, one, two, edge, inside, outside, partner, other)
+    )(filt, one, two, edge, inside, outside, partner, other)
     terms = lax.all_to_all(terms, FREQ, 0, 0)
 
     nearby = SHAPE[1] * SHAPE[3] * SHAPE[4]
@@ -703,11 +720,11 @@
     energies, beside = pl.pallas_call(
         relay_kernel,
         out_shape=(shape(far, 2, LANES), shape(4, 3, 8, LANES)),
-        in_specs=[SMEM] + whole(1),
+        in_specs=whole(1),
         out_specs=tuple(whole(2)),
         compiler_params=params(),
         name="relay",
-    )(place, near)
+    )(near)
     exchanged = lax.all_to_all(energies, FAR, 0, 0)
     pairs = []
     for i in range(strips):
@@ -718,12 +735,12 @@
     forward = pl.pallas_call(
         forward_kernel,
         out_shape=shape(5, 3, TAPS, LANES),
-        in_specs=[SMEM, SMEM] + whole(2),
+        in_specs=[SMEM] + whole(2),
         out_specs=whole(1)[0],
         compiler_params=params(),
         cost_estimate=pl.CostEstimate(flops=100000000, bytes_accessed=8000000, transcendentals=0),
         name="ahead",
-    )(place, spread_index, points, energies)
+    )(spread_index, points, energies)
 
     def scratch(count):
         return [
@@ -742,7 +759,7 @@
             shape(STEPS, 8, LANES),
             shape(1, LANES),
         ),
-        in_specs=[SMEM] + whole(4) + [HBM],
+        in_specs=whole(4) + [HBM],
         out_specs=tuple(whole(4)),
         scratch_shapes=[
             pltpu.VMEM((12, 3, 8, LANES), F32),
@@ -752,18 +769,18 @@
         + scratch(9),
         compiler_params=params(47),
         name="pass_one",
-    )(place, exchanged, near, beside, forward, tables)
+    )(exchanged, near, beside, forward, tables)
     parts = all_sum(parts)
     parts, descent, model = pl.pallas_call(
         second_kernel,
         out_shape=(shape(nearby, 1, LANES), shape(STEPS, 8, LANES), shape(STEPS, 8, LANES)),
-        in_specs=[SMEM] + whole(4) + [HBM],
+        in_specs=whole(4) + [HBM],
         out_specs=tuple(whole(3)),
         scratch_shapes=[pltpu.VMEM((6, 3, TAPS, LANES), F32), pltpu.SemaphoreType.DMA((6,))]
         + scratch(5),
         compiler_params=params(47),
         name="pass_two",
-    )(place, parts, energy, state, descent, tables)
+    )(parts, energy, state, descent, tables)
     parts = all_sum(parts)
     reflectivity, misfit = pl.pallas_call(
         last_kernel,

time: 136 us -> 133 us (0.978)
  Pallas kernels: 24.4 us -> 20.7 us
  waiting for transfers between devices: 10.8 us -> 12.2 us
  transfers between devices with their start and end apart: 5 -> 5, of which waited for: 3 -> 3; matrix products, arithmetic and copies ran while one was open for 1% -> 1% of each run, Pallas kernels for 7% -> 6%
where the time goes in v4:
time: 133 us
  blocking collectives  64 us (48%)
  starting transfers between devices  30.8 us (23%)
  Pallas kernels  20.7 us (16%)
  waiting for transfers between devices  12.2 us (9%)
  local copies, waits for them, and re-layouts  4.14 us (3%)
    all_to_all x2, blocking collectives, all_sum(): lax.all_to_all(jnp.broadcast_to(total[None], (ways, 1, LANES)), FAR, 0, 0)  25.6 us
    all_to_all x2, blocking collectives, all_sum(): near = lax.all_to_all(parts, NEAR, 0, 0)  22.6 us
    all_to_all x1, blocking collectives, local(): near = lax.all_to_all(payload, NEAR, 0, 0)  15.8 us
    all_to_all x1, starting transfers between devices, local(): terms = lax.all_to_all(terms, FREQ, 0, 0)  10.2 us
    ppermute x1, starting transfers between devices, local(): partner = lax.ppermute(inside, STRIP, swaps)  8.79 us
    all_to_all x1, waiting for transfers between devices, local(): terms = lax.all_to_all(terms, FREQ, 0, 0)  7.59 us
    all_to_all x1, starting transfers between devices, local(): exchanged = lax.all_to_all(energies, FAR, 0, 0)  6.75 us
    pallas_call x1, Pallas kernels, local(): pl.pallas_call(first_kernel, out_shape=(shape(nearby, 1, LANES), shape(10...  5.97 us
  transfers between devices with their start and end apart: 5, of which 3 were waited for; matrix products, arithmetic and copies ran while one was open for 1% of the time, Pallas kernels for 6%

profile of v4, /device:TPU:1, one launch (start us, length us, event | category | flops | bytes accessed | tf_op | source)
XLA Modules:
  0.0 132.7 jit_solution(11503628355308341546)
XLA Ops:
  0.6 0.0 copy-start
  0.6 0.9 copy-done
  1.5 0.0 copy-start.1
  1.5 0.9 copy-done.1
  2.4 0.0 copy-start.2
  2.4 0.8 copy-done.2
  3.3 0.0 copy-start.4
  3.3 0.5 pack.1
  3.8 8.8 %collective-permute-start = (f32[18,8,128]{2,1,0:T(8,128)S(1)}, f32[18,8,128]{2,1,0:T(8,128)S(1)}, u32[]{:S(2)}, u32[]{:S(2)}) collective-permute-start(f32[18,8,128]{2,1,0:T(8,128)S(1)} %get-tuple-element.32.inside), channel_id=1, source_target_pairs={{0,1},{1,0},{2,3},{3,2},{4,5},{5,4},{6,7},{7,6},{8,9},{9,8},{10,11... | collective-permute-start | bytes 221192 | tf_op jit(solution)/shard_map/ppermute | solution.py:654
  12.6 1.9 %collective-permute-start.1 = (f32[18,8,128]{2,1,0:T(8,128)S(1)}, f32[18,8,128]{2,1,0:T(8,128)S(1)}, u32[]{:S(2)}, u32[]{:S(2)}) collective-permute-start(f32[18,8,128]{2,1,0:T(8,128)S(1)} %get-tuple-element.33.outside), channel_id=1, source_target_pairs={{1,2},{2,1},{3,4},{4,3},{5,6},{6,5},{7,8},{8,7},{9,10},{10,9},{11,... | collective-permute-start | bytes 221192 | tf_op jit(solution)/shard_map/ppermute | solution.py:656
  14.5 0.0 copy-start.3
  14.5 0.7 copy-done.3
  15.2 2.0 %inner.1 = (f32[4,16,8,128]{3,2,1,0:T(8,128)S(1)}, f32[4,16,8,128]{3,2,1,0:T(8,128)S(1)}, f32[18,16,8,128]{3,2,1,0:T(8,128)S(1)}, f32[18,128]{1,0:T(8,128)S(1)}) custom-call(f32[4,16,8,128]{3,2,1,0:T(8,128)S(1)} %get-tuple-element.26.given, s32[16,8,128]{2,1,0:T(8,128)S(1)} %get-tuple-element.27.kinds, f32[1,8,2,9]{3,2,1,0:T(2,128)S(1)} %copy-done.3), custom_call_target="tpu_custom_call" | custom-call | flops 100000000 | bytes 8000000 | tf_op jit(solution)/shard_map/inner/pallas_call | solution.py:674
  17.2 0.0 collective-permute-done.partner
  17.3 1.0 collective-permute-done.1.other
  18.2 1.6 %edges.1 = f32[16,3,8,128]{3,2,1,0:T(8,128)} custom-call(f32[18,128]{1,0:T(8,128)S(1)} %get-tuple-element.28.filt, f32[4,16,8,128]{3,2,1,0:T(8,128)S(1)} %get-tuple-element.29.one, f32[4,16,8,128]{3,2,1,0:T(8,128)S(1)} %get-tuple-element.30.two, f32[18,16,8,128]{3,2,1,0:T(8,128)S(1)} %get-tuple-element.31.edge, f32[18,8,128]{2,1,0:T(8,128)S(1)} %get-tuple-element.32.inside, ...), custom_call_target="tpu_custom_call" | custom-call | tf_op jit(solution)/shard_map/edges/pallas_call | solution.py:695
  19.9 0.0 copy-start.5
  19.9 10.2 %all-to-all-start = ((f32[16,3,8,128]{3,2,1,0:T(8,128)}), f32[16,3,8,128]{3,2,1,0:T(8,128)S(1)}, u32[]{:S(2)}, u32[]{:S(2)}) async-start(f32[16,3,8,128]{3,2,1,0:T(8,128)} %edges.1), calls=%async_computation | async-start | bytes 393216 | tf_op jit(solution)/shard_map/all_to_all | solution.py:707
  30.1 0.0 copy-done.4
  30.1 0.2 fusion
  30.2 0.2 copy.20
  30.4 0.2 copy.21
  30.6 0.2 copy.22
  30.8 0.0 copy-done.5
  30.8 0.1 copy.18.index
  30.9 3.7 %tables.1 = (f32[24,3,240,128]{3,2,1,0:T(8,128)}, f32[8,128]{1,0:T(8,128)S(1)}) custom-call(s32[32,16]{1,0:T(8,128)S(1)} %copy.18.index, f32[240,32]{1,0:T(8,128)S(1)} %bitcast.8), custom_call_target="tpu_custom_call" | custom-call | flops 100000000 | bytes 8000000 | tf_op jit(solution)/shard_map/tables/pallas_call | solution.py:662
  34.6 7.6 %all-to-all-done.terms = f32[16,3,8,128]{3,2,1,0:T(8,128)S(1)} async-done(((f32[16,3,8,128]{3,2,1,0:T(8,128)}), f32[16,3,8,128]{3,2,1,0:T(8,128)S(1)}, u32[]{:S(2)}, u32[]{:S(2)}) %all-to-all-start) | async-done | bytes 196640 | tf_op jit(solution)/shard_map/all_to_all | solution.py:707
  42.2 0.6 stack.1
  42.8 15.8 %all_to_all.35.near = f32[16,3,8,128]{3,2,1,0:T(8,128)S(1)} all-to-all(f32[16,3,8,128]{3,2,1,0:T(8,128)S(1)} %get-tuple-element.36), channel_id=1, replica_groups=mesh['z'=8,'yh'=2,'x'=4,'yl'=4,'c'=2] {'yh','yl','c'}, dimensions={0} | all-to-all | bytes 393216 | tf_op jit(solution)/shard_map/all_to_all | solution.py:719
  58.6 0.6 relay.1
  59.2 6.8 %all-to-all-start.2 = ((f32[32,2,128]{2,1,0:T(2,128)}), f32[32,2,128]{2,1,0:T(2,128)S(1)}, u32[]{:S(2)}, u32[]{:S(2)}) async-start(f32[32,2,128]{2,1,0:T(2,128)} %get-tuple-element.37.after), calls=%async_computation.2 | async-start | bytes 65536 | tf_op jit(solution)/shard_map/all_to_all | solution.py:728
  66.0 3.1 %collective-permute-start.2 = (f32[4,3,8,128]{3,2,1,0:T(8,128)S(1)}, f32[4,3,8,128]{3,2,1,0:T(8,128)S(1)}, u32[]{:S(2)}, u32[]{:S(2)}) collective-permute-start(f32[4,3,8,128]{3,2,1,0:T(8,128)S(1)} %get-tuple-element.38), channel_id=1, source_target_pairs={{0,8},{1,9},{2,10},{3,11},{8,16},{9,17},{10,18},{11,19},{12,4},{13... | collective-permute-start | bytes 147464 | tf_op jit(solution)/shard_map/ppermute | solution.py:734
  69.1 1.9 %ahead.1.forward = f32[5,3,240,128]{3,2,1,0:T(8,128)S(1)} custom-call(s32[32,16]{1,0:T(8,128)S(1)} %copy.18.index, f32[240,32]{1,0:T(8,128)S(1)} %bitcast.9, f32[32,2,128]{2,1,0:T(2,128)} %get-tuple-element.37.after), custom_call_target="tpu_custom_call" | custom-call | flops 100000000 | bytes 8000000 | tf_op jit(solution)/shard_map/ahead/pallas_call | solution.py:735
  71.0 0.0 collective-permute-done.2.beside
  71.0 3.6 %all-to-all-done.2.energies = f32[32,2,128]{2,1,0:T(2,128)S(1)} async-done(((f32[32,2,128]{2,1,0:T(2,128)}), f32[32,2,128]{2,1,0:T(2,128)S(1)}, u32[]{:S(2)}, u32[]{:S(2)}) %all-to-all-start.2) | async-done | bytes 32800 | tf_op jit(solution)/shard_map/all_to_all | solution.py:728
  74.6 6.0 %pass_one.1 = (f32[16,1,128]{2,1,0:T(1,128)S(1)}, f32[10,3,8,128]{3,2,1,0:T(8,128)S(1)}, f32[2,8,128]{2,1,0:T(8,128)S(1)}, f32[1,128]{1,0:T(1,128)S(1)}) custom-call(f32[32,2,128]{2,1,0:T(2,128)S(1)} %all-to-all-done.2.energies, f32[16,3,8,128]{3,2,1,0:T(8,128)S(1)} %all_to_all.35.near, f32[4,3,8,128]{3,2,1,0:T(8,128)S(1)} %collective-permute-done.2.beside, ...), custom_call_target="tpu_custom_call" | custom-call | tf_op jit(solution)/shard_map/pass_one/pallas_call | solution.py:754
  80.6 11.1 %all_to_all.36 = f32[16,1,128]{2,1,0:T(1,128)S(1)} all-to-all(f32[16,1,128]{2,1,0:T(1,128)S(1)} %get-tuple-element.40), channel_id=1, replica_groups=mesh['z'=8,'yh'=2,'x'=4,'yl'=4,'c'=2] {'yh','yl','c'}, dimensions={0} | all-to-all | bytes 16384 | tf_op jit(solution)/shard_map/all_to_all | solution.py:621
  91.7 14.1 %all_to_all.37.parts = f32[32,1,128]{2,1,0:T(1,128)S(1)} all-to-all(f32[32,1,128]{2,1,0:T(1,128)S(1)} %broadcast_in_dim.4), channel_id=1, replica_groups=mesh['z'=8,'yh'=2,'x'=4,'yl'=4,'c'=2] {'z','x'}, dimensions={0} | all-to-all | bytes 32768 | tf_op jit(solution)/shard_map/all_to_all | solution.py:624
  105.8 3.0 %pass_two.1 = (f32[16,1,128]{2,1,0:T(1,128)S(1)}, f32[2,8,128]{2,1,0:T(8,128)S(1)}, f32[2,8,128]{2,1,0:T(8,128)S(1)}) custom-call(f32[32,1,128]{2,1,0:T(1,128)S(1)} %all_to_all.37.parts, f32[1,128]{1,0:T(1,128)S(1)} %get-tuple-element.41.energy, f32[10,3,8,128]{3,2,1,0:T(8,128)S(1)} %get-tuple-element.42.state, ...), custom_call_target="tpu_custom_call" | custom-call | tf_op jit(solution)/shard_map/pass_two/pallas_call | solution.py:774
  108.8 11.5 %all_to_all.38 = f32[16,1,128]{2,1,0:T(1,128)S(1)} all-to-all(f32[16,1,128]{2,1,0:T(1,128)S(1)} %get-tuple-element.44), channel_id=1, replica_groups=mesh['z'=8,'yh'=2,'x'=4,'yl'=4,'c'=2] {'yh','yl','c'}, dimensions={0} | all-to-all | bytes 16384 | tf_op jit(solution)/shard_map/all_to_all | solution.py:621
  120.4 11.6 %all_to_all.39.parts = f32[32,1,128]{2,1,0:T(1,128)S(1)} all-to-all(f32[32,1,128]{2,1,0:T(1,128)S(1)} %broadcast_in_dim.5), channel_id=1, replica_groups=mesh['z'=8,'yh'=2,'x'=4,'yl'=4,'c'=2] {'z','x'}, dimensions={0} | all-to-all | bytes 32768 | tf_op jit(solution)/shard_map/all_to_all | solution.py:624
  132.0 0.8 last.1
  (7 shorter events, 0.2 us)
Async XLA Ops:
  0.6 0.9 copy-start
  1.5 0.9 copy-start.1
  2.4 0.8 copy-start.2
  3.3 26.8 %copy-start.4 = (f32[16,2,15,15]{0,1,3,2:T(2,128)S(1)}, f32[16,2,15,15]{0,1,3,2:T(2,128)}, u32[]{:S(2)}) copy-start(f32[16,2,15,15]{0,1,3,2:T(2,128)} %param.10) | copy-start | bytes 86404
  3.8 13.5 %collective-permute-start = (f32[18,8,128]{2,1,0:T(8,128)S(1)}, f32[18,8,128]{2,1,0:T(8,128)S(1)}, u32[]{:S(2)}, u32[]{:S(2)}) collective-permute-start(f32[18,8,128]{2,1,0:T(8,128)S(1)} %get-tuple-element.32.inside), channel_id=1, source_target_pairs={{0,1},{1,0},{2,3},{3,2},{4,5},{5,4},{6,7},{7,6},{8,9},{9,8},{10,11... | collective-permute-start | bytes 221192 | tf_op jit(solution)/shard_map/ppermute | solution.py:654
  12.6 5.7 %collective-permute-start.1 = (f32[18,8,128]{2,1,0:T(8,128)S(1)}, f32[18,8,128]{2,1,0:T(8,128)S(1)}, u32[]{:S(2)}, u32[]{:S(2)}) collective-permute-start(f32[18,8,128]{2,1,0:T(8,128)S(1)} %get-tuple-element.33.outside), channel_id=1, source_target_pairs={{1,2},{2,1},{3,4},{4,3},{5,6},{6,5},{7,8},{8,7},{9,10},{10,9},{11,... | collective-permute-start | bytes 221192 | tf_op jit(solution)/shard_map/ppermute | solution.py:656
  14.5 0.7 copy-start.3
  19.9 10.9 %copy-start.5 = (s32[32,16]{0,1:T(8,128)S(1)}, s32[32,16]{0,1:T(8,128)}, u32[]{:S(2)}) copy-start(s32[32,16]{0,1:T(8,128)} %param.11) | copy-start | bytes 6148
  19.9 22.3 %all-to-all-start = ((f32[16,3,8,128]{3,2,1,0:T(8,128)}), f32[16,3,8,128]{3,2,1,0:T(8,128)S(1)}, u32[]{:S(2)}, u32[]{:S(2)}) async-start(f32[16,3,8,128]{3,2,1,0:T(8,128)} %edges.1), calls=%async_computation | async-start | bytes 393216 | tf_op jit(solution)/shard_map/all_to_all | solution.py:707
  59.2 15.5 %all-to-all-start.2 = ((f32[32,2,128]{2,1,0:T(2,128)}), f32[32,2,128]{2,1,0:T(2,128)S(1)}, u32[]{:S(2)}, u32[]{:S(2)}) async-start(f32[32,2,128]{2,1,0:T(2,128)} %get-tuple-element.37.after), calls=%async_computation.2 | async-start | bytes 65536 | tf_op jit(solution)/shard_map/all_to_all | solution.py:728
  66.0 5.1 %collective-permute-start.2 = (f32[4,3,8,128]{3,2,1,0:T(8,128)S(1)}, f32[4,3,8,128]{3,2,1,0:T(8,128)S(1)}, u32[]{:S(2)}, u32[]{:S(2)}) collective-permute-start(f32[4,3,8,128]{3,2,1,0:T(8,128)S(1)} %get-tuple-element.38), channel_id=1, source_target_pairs={{0,8},{1,9},{2,10},{3,11},{8,16},{9,17},{10,18},{11,19},{12,4},{13... | collective-permute-start | bytes 147464 | tf_op jit(solution)/shard_map/ppermute | solution.py:734
